TPU v7x, 128 devices: a whole 4x4x4 slice. The times are simulated.
128 devices in a mesh: gx: 16 (over x, z), gy: 8 (over y, core).
Axes of the slice: x: 4, y: 4, z: 4, core: 2. Of those that a mesh axis runs over, the one named last changes fastest.
Arguments:
- right_side: float32 [64, 64, 512], P('gx', 'gy'), may hold values from -8 to 8
- permeability: float32 [64, 64, 512], P('gx', 'gy'), may hold values from 0.001 to 1000
- accumulation: float32 [64, 64, 512], P('gx', 'gy'), may hold values from 0.001 to 0.1
- active: int32 [64, 64, 512], P('gx', 'gy'), may hold values 0 or 1
- fault_local: int32 [128, 128, 128], P(('gx', 'gy')), may hold values from 0 to 16383
- fault_remote: int32 [128, 128, 128], P(('gx', 'gy')), may hold values from 0 to 16383
- fault_count: int32 [128, 128], P(('gx', 'gy')), may hold values from 0 to 128, as said below
- fault_mult: float32 [128, 128, 128], P(('gx', 'gy')), may hold values from 0.3 to 1
- low_bound: float32 [1], replicated, may hold values from 0.02 to 0.1
- high_bound: float32 [1], replicated, may hold values from 1.8 to 2
Outputs:
- correction: float32 [64, 64, 512], P('gx', 'gy')
- residual: float32 [64, 64, 512], P('gx', 'gy')
Inputs may be any that keep to these rules, and one draw needn't show every extreme that they name: `fault_local`: a cell of the owner's block, numbered with layers fastest; slots at or beyond the block's count carry no connection. `fault_remote`: a cell of the remote owner's block, numbered likewise. `fault_count`: some block is full.
All inputs are finite; a program needn't handle non-finite values. No bound on the sum of `active` on one device may be relied on, other than what follows from the above.
Results may differ from a plain program's by a relative error of at most 0.000021.
Values sent between devices are 32-bit elements; how exact they have to be, the bound alone decides.
A program may use at most 64 MiB of HBM per device.

v0:
```python
import jax
import jax.numpy as jnp
from jax import lax
from jax.sharding import PartitionSpec as P

ITERS = 3


def padded_2(cells, sides, width):
    for axis, dim in sides:
        count = lax.axis_size(axis)
        ends = count - 1
        head = lax.slice_in_dim(cells, 0, width, axis=dim)
        tail = lax.slice_in_dim(cells, cells.shape[dim] - width, cells.shape[dim], axis=dim)
        cells = jnp.concatenate(
            [
                lax.ppermute(tail, axis, [(i, (i + 1) % count) for i in range(ends)]),
                cells,
                lax.ppermute(head, axis, [((i + 1) % count, i) for i in range(ends)]),
            ],
            axis=dim,
        )
    return cells


def harmonic(k_one, a_one, k_two, a_two, factor):
    return factor * (2.0 * (k_one * k_two)) / (k_one + k_two) * (a_one * a_two)


def fault_move(values):
    return tuple(lax.all_to_all(values, ("gx", "gy"), split_axis=1, concat_axis=1, tiled=True))


def on_device(
    right_side,
    permeability,
    accumulation,
    active,
    fault_local,
    fault_remote,
    fault_count,
    fault_mult,
    low_bound,
    high_bound,
):
    width_x, width_y, layers = right_side.shape
    cells = width_x * width_y * layers
    act = active.astype(jnp.float32)
    props = padded_2(jnp.stack([permeability, act]), (("gx", 1), ("gy", 2)), 1)
    perm_pad = props[0]
    act_pad = props[1]
    east = harmonic(permeability, act, perm_pad[2:, 1:-1], act_pad[2:, 1:-1], 1.0)
    west = harmonic(permeability, act, perm_pad[:-2, 1:-1], act_pad[:-2, 1:-1], 1.0)
    north = harmonic(permeability, act, perm_pad[1:-1, 2:], act_pad[1:-1, 2:], 1.0)
    south = harmonic(permeability, act, perm_pad[1:-1, :-2], act_pad[1:-1, :-2], 1.0)
    vertical = harmonic(
        permeability[:, :, :-1], act[:, :, :-1], permeability[:, :, 1:], act[:, :, 1:], 0.8
    )
    upper = jnp.pad(vertical, ((0, 0), (0, 0), (0, 1)))
    lower = jnp.pad(vertical, ((0, 0), (0, 0), (1, 0)))
    requests = lax.all_to_all(fault_remote, ("gx", "gy"), split_axis=1, concat_axis=1, tiled=True)
    perm_flat = permeability.reshape(-1)
    act_flat = act.reshape(-1)
    remote_perm, remote_act = fault_move((perm_flat[requests], act_flat[requests]))
    slots = lax.broadcasted_iota(jnp.int32, fault_local.shape, 2)
    valid = (slots < fault_count[:, :, None]).astype(jnp.float32)
    fault_trans = (
        harmonic(perm_flat[fault_local], act_flat[fault_local], remote_perm, remote_act, 1.0)
        * fault_mult
        * valid
    )
    (incoming,) = fault_move((fault_trans,))
    local_list = fault_local.reshape(-1)
    asked_list = requests.reshape(-1)
    fault_diag = (
        jnp.zeros(cells, jnp.float32)
        .at[local_list]
        .add(fault_trans.reshape(-1))
        .at[asked_list]
        .add(incoming.reshape(-1))
    )
    diag_acc = jnp.where(active != 0, accumulation, jnp.float32(1.0))
    diagonal = (
        diag_acc
        + east
        + west
        + north
        + south
        + upper
        + lower
        + fault_diag.reshape(right_side.shape)
    )
    low = low_bound[0]
    high = high_bound[0]
    theta = (high + low) / 2.0
    delta = (high - low) / 2.0
    sigma = theta / delta
    rho = 1.0 / sigma
    correction = jnp.zeros_like(right_side)
    residual = right_side
    step = residual / diagonal / theta
    for count in range(ITERS):
        correction = correction + step
        padded = padded_2(step, (("gx", 0), ("gy", 1)), 1)
        result = diag_acc * step
        result = result + east * (step - padded[2:, 1:-1]) + west * (step - padded[:-2, 1:-1])
        result = result + north * (step - padded[1:-1, 2:]) + south * (step - padded[1:-1, :-2])
        above = jnp.pad(step[:, :, 1:], ((0, 0), (0, 0), (0, 1)))
        below = jnp.pad(step[:, :, :-1], ((0, 0), (0, 0), (1, 0)))
        result = result + upper * (step - above) + lower * (step - below)
        flat = step.reshape(-1)
        local_values = flat[fault_local]
        asked_values = flat[requests]
        (remote_values,) = fault_move((asked_values,))
        own_flux = fault_trans * (local_values - remote_values)
        (returned,) = fault_move((own_flux,))
        back_flux = -returned
        extra = (
            jnp.zeros(cells, jnp.float32)
            .at[local_list]
            .add(own_flux.reshape(-1))
            .at[asked_list]
            .add(back_flux.reshape(-1))
        )
        residual = residual - (result + extra.reshape(step.shape))
        if count + 1 < ITERS:
            rho_new = 1.0 / (2.0 * sigma - rho)
            step = rho_new * rho * step + 2.0 * rho_new / delta * (residual / diagonal)
            rho = rho_new
    return (correction, residual)


def solution(mesh):
    in_specs = (
        P("gx", "gy", None),
        P("gx", "gy", None),
        P("gx", "gy", None),
        P("gx", "gy", None),
        P(("gx", "gy"), None, None),
        P(("gx", "gy"), None, None),
        P(("gx", "gy"), None),
        P(("gx", "gy"), None, None),
        P(),
        P(),
    )
    out_specs = (P("gx", "gy", None), P("gx", "gy", None))
    return jax.shard_map(
        on_device, mesh=mesh, in_specs=in_specs, out_specs=out_specs, check_vma=False
    )
```

profile of v0, /device:TPU:1, one launch (start us, length us, event | category | flops | bytes accessed | tf_op | source)
XLA Modules:
  0.0 2113.4 jit_solution(13325088188543283477)
XLA Ops:
  0.6 11.5 all-to-all-start
  19.7 90.5 %gather_fusion = f32[16384]{0:T(1024)S(1)} fusion(f32[16384]{0:T(1024)S(1)} %bitcast.66, s32[16384]{0:T(1024)S(1)} %broadcast_clamp_fusion.1), kind=kCustom, calls=%fused_computation | custom fusion | bytes 196608 | tf_op jit(solution)/shard_map/gather | solution.py:68
  110.2 90.5 %gather_fusion.2 = f32[16384]{0:T(1024)S(1)} fusion(f32[16384]{0:T(1024)S(1)} %bitcast.64, s32[16384]{0:T(1024)S(1)} %broadcast_clamp_fusion.1), kind=kCustom, calls=%fused_computation.2 | custom fusion | bytes 196608 | tf_op jit(solution)/shard_map/gather | solution.py:68
  206.6 160.6 %gather_fusion.1 = f32[16384]{0:T(1024)} fusion(f32[16384]{0:T(1024)S(1)} %bitcast.67, s32[16384]{0:T(1024)S(1)} %broadcast_clamp_fusion), kind=kCustom, calls=%fused_computation.1 | custom fusion | bytes 196608 | tf_op jit(solution)/shard_map/gather | solution.py:64
  367.2 10.9 all-to-all-start.1
  378.1 160.6 %gather_fusion.3 = f32[16384]{0:T(1024)} fusion(f32[16384]{0:T(1024)S(1)} %bitcast.65, s32[16384]{0:T(1024)S(1)} %broadcast_clamp_fusion), kind=kCustom, calls=%fused_computation.3 | custom fusion | bytes 196608 | tf_op jit(solution)/shard_map/gather | solution.py:64
  538.7 9.8 all-to-all-start.2
  548.6 9.4 all-to-all-done.2
  559.4 4.6 all-to-all-start.3
  564.1 86.1 %scatter_custom_fusion = f32[16384]{0:T(1024)S(1)} fusion(s32[16384]{0:T(1024)S(1)} %bitcast.105, f32[16384]{0:T(1024)} %bitcast.19, f32[]{:T(128)} %constant.11.clone.1), kind=kCustom, calls=%fused_computation.127 | custom fusion | flops 16384 | bytes 66048 | tf_op jit(solution)/shard_map/scatter-add | solution.py:78
  650.2 87.9 %scatter_fusion = f32[16384]{0:T(1024)S(1)} fusion(f32[16384]{0:T(1024)S(1)} %scatter_custom_fusion, s32[16384]{0:T(1024)S(1)} %bitcast.81, f32[16384]{0:T(1024)S(1)} %bitcast.87), kind=kCustom, calls=%fused_computation.11 | custom fusion | flops 16384 | bytes 262144 | tf_op jit(solution)/shard_map/scatter-add | solution.py:80
  744.0 160.6 %gather_fusion.5 = f32[16384]{0:T(1024)} fusion(f32[16384]{0:T(1024)S(1)} %bitcast.70, s32[16384]{0:T(1024)S(1)} %broadcast_clamp_fusion), kind=kCustom, calls=%fused_computation.5 | custom fusion | bytes 196608 | tf_op jit(solution)/shard_map/gather | solution.py:113
  904.6 90.5 %gather_fusion.4 = f32[16384]{0:T(1024)S(1)} fusion(f32[16384]{0:T(1024)S(1)} %bitcast.71, s32[16384]{0:T(1024)S(1)} %broadcast_clamp_fusion.1), kind=kCustom, calls=%fused_computation.4 | custom fusion | bytes 196608 | tf_op jit(solution)/shard_map/gather | solution.py:112
  995.2 10.9 all-to-all-start.4
  1011.7 3.8 all-to-all-done.4
  1017.0 5.7 all-to-all-start.5
  1022.8 86.1 %scatter_custom_fusion.2 = f32[16384]{0:T(1024)S(1)} fusion(s32[16384]{0:T(1024)S(1)} %bitcast.106, f32[16384]{0:T(1024)} %bitcast.27, f32[]{:T(128)} %constant.11.clone.1), kind=kCustom, calls=%fused_computation.125 | custom fusion | flops 16384 | bytes 66048 | tf_op jit(solution)/shard_map/scatter-add | solution.py:121
  1109.0 88.1 %scatter_fusion.1 = f32[16384]{0:T(1024)S(1)} fusion(f32[16384]{0:T(1024)S(1)} %scatter_custom_fusion.2, s32[16384]{0:T(1024)S(1)} %bitcast.82, f32[16384]{0:T(1024)S(1)} %bitcast.89), kind=kCustom, calls=%fused_computation.13 | custom fusion | flops 16384 | bytes 262144 | tf_op jit(solution)/shard_map/scatter-add | solution.py:123
  1202.0 160.6 %gather_fusion.7 = f32[16384]{0:T(1024)} fusion(f32[16384]{0:T(1024)S(1)} %bitcast.72, s32[16384]{0:T(1024)S(1)} %broadcast_clamp_fusion), kind=kCustom, calls=%fused_computation.7 | custom fusion | bytes 196608 | tf_op jit(solution)/shard_map/gather | solution.py:113
  1362.6 90.5 %gather_fusion.6 = f32[16384]{0:T(1024)S(1)} fusion(f32[16384]{0:T(1024)S(1)} %bitcast.73, s32[16384]{0:T(1024)S(1)} %broadcast_clamp_fusion.1), kind=kCustom, calls=%fused_computation.6 | custom fusion | bytes 196608 | tf_op jit(solution)/shard_map/gather | solution.py:112
  1453.2 10.9 all-to-all-start.6
  1469.7 3.8 all-to-all-done.6
  1475.0 5.7 all-to-all-start.7
  1480.8 86.1 %scatter_custom_fusion.4 = f32[16384]{0:T(1024)S(1)} fusion(s32[16384]{0:T(1024)S(1)} %bitcast.107, f32[16384]{0:T(1024)} %bitcast.31, f32[]{:T(128)} %constant.11.clone.1), kind=kCustom, calls=%fused_computation.123 | custom fusion | flops 16384 | bytes 66048 | tf_op jit(solution)/shard_map/scatter-add | solution.py:121
  1567.0 87.9 %scatter_fusion.2 = f32[16384]{0:T(1024)S(1)} fusion(f32[16384]{0:T(1024)S(1)} %scatter_custom_fusion.4, s32[16384]{0:T(1024)S(1)} %bitcast.83, f32[16384]{0:T(1024)S(1)} %bitcast.90), kind=kCustom, calls=%fused_computation.15 | custom fusion | flops 16384 | bytes 262144 | tf_op jit(solution)/shard_map/scatter-add | solution.py:123
  1660.4 160.1 %gather_fusion.9 = f32[16384]{0:T(1024)} fusion(f32[16384]{0:T(1024)S(1)} %bitcast.68, s32[16384]{0:T(1024)S(1)} %broadcast_clamp_fusion), kind=kCustom, calls=%fused_computation.9 | custom fusion | bytes 196608 | tf_op jit(solution)/shard_map/gather | solution.py:113
  1820.4 90.5 %gather_fusion.8 = f32[16384]{0:T(1024)S(1)} fusion(f32[16384]{0:T(1024)S(1)} %bitcast.69, s32[16384]{0:T(1024)S(1)} %broadcast_clamp_fusion.1), kind=kCustom, calls=%fused_computation.8 | custom fusion | bytes 196608 | tf_op jit(solution)/shard_map/gather | solution.py:112
  1911.0 10.9 all-to-all-start.8
  1927.5 3.9 all-to-all-done.8
  1932.8 5.7 all-to-all-start.9
  1938.6 86.1 %scatter_custom_fusion.6 = f32[16384]{0:T(1024)S(1)} fusion(s32[16384]{0:T(1024)S(1)} %bitcast.108, f32[16384]{0:T(1024)} %bitcast.35, f32[]{:T(128)} %constant.11.clone.1), kind=kCustom, calls=%fused_computation.121 | custom fusion | flops 16384 | bytes 66048 | tf_op jit(solution)/shard_map/scatter-add | solution.py:121
  2024.8 87.9 %scatter_fusion.3 = f32[16384]{0:T(1024)S(1)} fusion(f32[16384]{0:T(1024)S(1)} %scatter_custom_fusion.6, s32[16384]{0:T(1024)S(1)} %bitcast.84, f32[16384]{0:T(1024)S(1)} %bitcast.88), kind=kCustom, calls=%fused_computation.17 | custom fusion | flops 16384 | bytes 262144 | tf_op jit(solution)/shard_map/scatter-add | solution.py:123
  (97 shorter events, 51.9 us)
Async XLA Ops:
  0.6 11.5 copy-start.3
  0.6 205.8 %all-to-all-start = ((s32[1,128,128]{2,0,1:T(1,128)}), s32[1,128,128]{2,0,1:T(1,128)S(1)}, u32[]{:S(2)}, u32[]{:S(2)}) async-start(s32[1,128,128]{2,0,1:T(1,128)} %bitcast.104), calls=%async_computation | async-start | bytes 131072 | tf_op jit(solution)/shard_map/all_to_all | solution.py:61
  12.2 0.8 copy-start
  13.0 4.9 copy-start.1
  13.0 187.8 %collective-permute-start = (f32[2,1,8,512]{3,2,1,0:T(8,128)S(1)}, f32[2,1,8,512]{3,2,1,0:T(8,128)S(1)}, u32[]{:S(2)}, u32[]{:S(2)}) collective-permute-start(f32[2,1,8,512]{3,2,1,0:T(8,128)S(1)} %get-tuple-element.18), channel_id=1, source_target_pairs={{0,8},{8,16},{16,24},{24,32},{32,40},{40,48},{48,56},{56,64},{64,7... | collective-permute-start | bytes 98312 | tf_op jit(solution)/shard_map/ppermute | solution.py:17
  16.6 184.2 %collective-permute-start.1 = (f32[2,1,8,512]{3,2,1,0:T(8,128)S(1)}, f32[2,1,8,512]{3,2,1,0:T(8,128)S(1)}, u32[]{:S(2)}, u32[]{:S(2)}) collective-permute-start(f32[2,1,8,512]{3,2,1,0:T(8,128)S(1)} %get-tuple-element.19), channel_id=1, source_target_pairs={{8,0},{16,8},{24,16},{32,24},{40,32},{48,40},{56,48},{64,56},{72,6... | collective-permute-start | bytes 98312 | tf_op jit(solution)/shard_map/ppermute | solution.py:19
  200.8 177.2 %collective-permute-start.2 = (f32[2,6,1,512]{3,2,1,0:T(1,128)S(1)}, f32[2,6,1,512]{3,2,1,0:T(1,128)S(1)}, u32[]{:S(2)}, u32[]{:S(2)}) collective-permute-start(f32[2,6,1,512]{3,2,1,0:T(1,128)S(1)} %get-tuple-element.16), channel_id=1, source_target_pairs={{0,1},{1,2},{2,3},{3,4},{4,5},{5,6},{6,7},{8,9},{9,10},{10,11},{11... | collective-permute-start | bytes 73736 | tf_op jit(solution)/shard_map/ppermute | solution.py:17
  204.5 173.5 %collective-permute-start.3 = (f32[2,6,1,512]{3,2,1,0:T(1,128)S(1)}, f32[2,6,1,512]{3,2,1,0:T(1,128)S(1)}, u32[]{:S(2)}, u32[]{:S(2)}) collective-permute-start(f32[2,6,1,512]{3,2,1,0:T(1,128)S(1)} %get-tuple-element.17), channel_id=1, source_target_pairs={{1,0},{2,1},{3,2},{4,3},{5,4},{6,5},{7,6},{9,8},{10,9},{11,10},{12... | collective-permute-start | bytes 73736 | tf_op jit(solution)/shard_map/ppermute | solution.py:19
  367.2 171.6 %all-to-all-start.1 = ((f32[1,128,128]{2,0,1:T(1,128)}), f32[1,128,128]{2,0,1:T(1,128)S(1)}, u32[]{:S(2)}, u32[]{:S(2)}) async-start(f32[1,128,128]{2,0,1:T(1,128)} %bitcast.15), calls=%async_computation.1 | async-start | bytes 131072 | tf_op jit(solution)/shard_map/all_to_all | solution.py:31
  538.7 19.2 all-to-all-start.2
  548.5 9.4 copy-start.5
  559.4 90.8 %all-to-all-start.3 = ((f32[1,128,128]{2,0,1:T(1,128)}), f32[1,128,128]{2,0,1:T(1,128)S(1)}, u32[]{:S(2)}, u32[]{:S(2)}) async-start(f32[1,128,128]{2,0,1:T(1,128)} %compare_select_fusion.3), calls=%async_computation.3 | async-start | bytes 131072 | tf_op jit(solution)/shard_map/all_to_all | solution.py:31
  738.1 0.8 copy-start.2
  738.1 0.9 copy-start.4
  739.1 267.0 %collective-permute-start.5 = (f32[1,8,512]{2,1,0:T(8,128)S(1)}, f32[1,8,512]{2,1,0:T(8,128)S(1)}, u32[]{:S(2)}, u32[]{:S(2)}) collective-permute-start(f32[1,8,512]{2,1,0:T(8,128)S(1)} %get-tuple-element.34), channel_id=1, source_target_pairs={{0,8},{8,16},{16,24},{24,32},{32,40},{40,48},{48,56},{56,64},{64,7... | collective-permute-start | bytes 49160 | tf_op jit(solution)/shard_map/ppermute | solution.py:17
  742.5 263.6 %collective-permute-start.4 = (f32[1,8,512]{2,1,0:T(8,128)S(1)}, f32[1,8,512]{2,1,0:T(8,128)S(1)}, u32[]{:S(2)}, u32[]{:S(2)}) collective-permute-start(f32[1,8,512]{2,1,0:T(8,128)S(1)} %get-tuple-element.35), channel_id=1, source_target_pairs={{8,0},{16,8},{24,16},{32,24},{40,32},{48,40},{56,48},{64,56},{72,6... | collective-permute-start | bytes 49160 | tf_op jit(solution)/shard_map/ppermute | solution.py:19
  995.2 20.3 all-to-all-start.4
  1006.1 190.9 %collective-permute-start.6 = (f32[6,1,512]{2,1,0:T(1,128)S(1)}, f32[6,1,512]{2,1,0:T(1,128)S(1)}, u32[]{:S(2)}, u32[]{:S(2)}) collective-permute-start(f32[6,1,512]{2,1,0:T(1,128)S(1)} %get-tuple-element.24), channel_id=1, source_target_pairs={{1,0},{2,1},{3,2},{4,3},{5,4},{6,5},{7,6},{9,8},{10,9},{11,10},{12... | collective-permute-start | bytes 36872 | tf_op jit(solution)/shard_map/ppermute | solution.py:19
  1009.1 187.9 %collective-permute-start.7 = (f32[6,1,512]{2,1,0:T(1,128)S(1)}, f32[6,1,512]{2,1,0:T(1,128)S(1)}, u32[]{:S(2)}, u32[]{:S(2)}) collective-permute-start(f32[6,1,512]{2,1,0:T(1,128)S(1)} %get-tuple-element.25), channel_id=1, source_target_pairs={{0,1},{1,2},{2,3},{3,4},{4,5},{5,6},{6,7},{8,9},{9,10},{10,11},{11... | collective-permute-start | bytes 36872 | tf_op jit(solution)/shard_map/ppermute | solution.py:17
  1017.0 91.9 %all-to-all-start.5 = ((f32[1,128,128]{2,0,1:T(1,128)}), f32[1,128,128]{2,0,1:T(1,128)S(1)}, u32[]{:S(2)}, u32[]{:S(2)}) async-start(f32[1,128,128]{2,0,1:T(1,128)} %bitcast.55), calls=%async_computation.5 | async-start | bytes 131072 | tf_op jit(solution)/shard_map/all_to_all | solution.py:31
  1197.2 266.9 %collective-permute-start.9 = (f32[1,8,512]{2,1,0:T(8,128)S(1)}, f32[1,8,512]{2,1,0:T(8,128)S(1)}, u32[]{:S(2)}, u32[]{:S(2)}) collective-permute-start(f32[1,8,512]{2,1,0:T(8,128)S(1)} %get-tuple-element.30), channel_id=1, source_target_pairs={{0,8},{8,16},{16,24},{24,32},{32,40},{40,48},{48,56},{56,64},{64,7... | collective-permute-start | bytes 49160 | tf_op jit(solution)/shard_map/ppermute | solution.py:17
  1200.6 263.5 %collective-permute-start.8 = (f32[1,8,512]{2,1,0:T(8,128)S(1)}, f32[1,8,512]{2,1,0:T(8,128)S(1)}, u32[]{:S(2)}, u32[]{:S(2)}) collective-permute-start(f32[1,8,512]{2,1,0:T(8,128)S(1)} %get-tuple-element.31), channel_id=1, source_target_pairs={{8,0},{16,8},{24,16},{32,24},{40,32},{48,40},{56,48},{64,56},{72,6... | collective-permute-start | bytes 49160 | tf_op jit(solution)/shard_map/ppermute | solution.py:19
  1453.2 20.3 all-to-all-start.6
  1464.1 190.7 %collective-permute-start.10 = (f32[6,1,512]{2,1,0:T(1,128)S(1)}, f32[6,1,512]{2,1,0:T(1,128)S(1)}, u32[]{:S(2)}, u32[]{:S(2)}) collective-permute-start(f32[6,1,512]{2,1,0:T(1,128)S(1)} %get-tuple-element.22), channel_id=1, source_target_pairs={{1,0},{2,1},{3,2},{4,3},{5,4},{6,5},{7,6},{9,8},{10,9},{11,10},{12... | collective-permute-start | bytes 36872 | tf_op jit(solution)/shard_map/ppermute | solution.py:19
  1467.1 187.8 %collective-permute-start.11 = (f32[6,1,512]{2,1,0:T(1,128)S(1)}, f32[6,1,512]{2,1,0:T(1,128)S(1)}, u32[]{:S(2)}, u32[]{:S(2)}) collective-permute-start(f32[6,1,512]{2,1,0:T(1,128)S(1)} %get-tuple-element.23), channel_id=1, source_target_pairs={{0,1},{1,2},{2,3},{3,4},{4,5},{5,6},{6,7},{8,9},{9,10},{10,11},{11... | collective-permute-start | bytes 36872 | tf_op jit(solution)/shard_map/ppermute | solution.py:17
  1475.0 91.9 %all-to-all-start.7 = ((f32[1,128,128]{2,0,1:T(1,128)}), f32[1,128,128]{2,0,1:T(1,128)S(1)}, u32[]{:S(2)}, u32[]{:S(2)}) async-start(f32[1,128,128]{2,0,1:T(1,128)} %bitcast.59), calls=%async_computation.7 | async-start | bytes 131072 | tf_op jit(solution)/shard_map/all_to_all | solution.py:31
  1655.6 266.2 %collective-permute-start.13 = (f32[1,8,512]{2,1,0:T(8,128)S(1)}, f32[1,8,512]{2,1,0:T(8,128)S(1)}, u32[]{:S(2)}, u32[]{:S(2)}) collective-permute-start(f32[1,8,512]{2,1,0:T(8,128)S(1)} %get-tuple-element.28), channel_id=1, source_target_pairs={{0,8},{8,16},{16,24},{24,32},{32,40},{40,48},{48,56},{56,64},{64,7... | collective-permute-start | bytes 49160 | tf_op jit(solution)/shard_map/ppermute | solution.py:17
  1659.0 262.8 %collective-permute-start.12 = (f32[1,8,512]{2,1,0:T(8,128)S(1)}, f32[1,8,512]{2,1,0:T(8,128)S(1)}, u32[]{:S(2)}, u32[]{:S(2)}) collective-permute-start(f32[1,8,512]{2,1,0:T(8,128)S(1)} %get-tuple-element.29), channel_id=1, source_target_pairs={{8,0},{16,8},{24,16},{32,24},{40,32},{48,40},{56,48},{64,56},{72,6... | collective-permute-start | bytes 49160 | tf_op jit(solution)/shard_map/ppermute | solution.py:19
  1911.0 20.4 all-to-all-start.8
  1921.9 190.7 %collective-permute-start.14 = (f32[6,1,512]{2,1,0:T(1,128)S(1)}, f32[6,1,512]{2,1,0:T(1,128)S(1)}, u32[]{:S(2)}, u32[]{:S(2)}) collective-permute-start(f32[6,1,512]{2,1,0:T(1,128)S(1)} %get-tuple-element.20), channel_id=1, source_target_pairs={{1,0},{2,1},{3,2},{4,3},{5,4},{6,5},{7,6},{9,8},{10,9},{11,10},{12... | collective-permute-start | bytes 36872 | tf_op jit(solution)/shard_map/ppermute | solution.py:19
  1924.9 187.8 %collective-permute-start.15 = (f32[6,1,512]{2,1,0:T(1,128)S(1)}, f32[6,1,512]{2,1,0:T(1,128)S(1)}, u32[]{:S(2)}, u32[]{:S(2)}) collective-permute-start(f32[6,1,512]{2,1,0:T(1,128)S(1)} %get-tuple-element.21), channel_id=1, source_target_pairs={{0,1},{1,2},{2,3},{3,4},{4,5},{5,6},{6,7},{8,9},{9,10},{10,11},{11... | collective-permute-start | bytes 36872 | tf_op jit(solution)/shard_map/ppermute | solution.py:17
  1932.8 91.8 %all-to-all-start.9 = ((f32[1,128,128]{2,0,1:T(1,128)}), f32[1,128,128]{2,0,1:T(1,128)S(1)}, u32[]{:S(2)}, u32[]{:S(2)}) async-start(f32[1,128,128]{2,0,1:T(1,128)} %bitcast.63), calls=%async_computation.9 | async-start | bytes 131072 | tf_op jit(solution)/shard_map/all_to_all | solution.py:31
  (1 other events, 0.7 us)
where the time goes:
time: 2110 us
  local copies, waits for them, and re-layouts  1260 us (60%)
  other arithmetic  704 us (33%)
  starting transfers between devices  128 us (6%)
    scatter-add x6, other arithmetic, on_device(): extra = jnp.zeros(cells, jnp.float32).at[local_list].add(own_flux.reshape...  522 us
    gather x3, local copies, waits for them, and re-layouts, on_device(): asked_values = flat[requests]  481 us
    gather x3, local copies, waits for them, and re-layouts, on_device(): local_values = flat[fault_local]  272 us
    scatter-add x2, other arithmetic, on_device(): fault_diag = jnp.zeros(cells, jnp.float32).at[local_list].add(fault_trans...  174 us
    gather x1, local copies, waits for them, and re-layouts, on_device(): perm_flat[requests]  161 us
    gather x1, local copies, waits for them, and re-layouts, on_device(): act_flat[requests]  161 us
    gather x1, local copies, waits for them, and re-layouts, on_device(): act_flat[fault_local]  90.5 us
    gather x1, local copies, waits for them, and re-layouts, on_device(): perm_flat[fault_local]  90.5 us
  transfers between devices with their start and end apart: 26, of which 4 were waited for; matrix products, arithmetic and copies ran while one was open for 88% of the time, Pallas kernels for 0%

commit v1 on v0

v1 whole, which is shorter than its diff:
```python
import functools

import jax
import jax.numpy as jnp
from jax import lax
from jax.experimental import pallas as pl
from jax.experimental.pallas import tpu as pltpu
from jax.sharding import PartitionSpec as P

ITERS = 3
PEERS = 128
CHUNKS = 4
PER = PEERS // CHUNKS
LANES = 128
MESH = pl.DeviceIdType.MESH
F32 = jnp.float32
BF16 = jnp.bfloat16


def harmonic(k_one, k_two, factor):
    total = k_one + k_two
    safe = jnp.where(total > 0.0, total, 1.0)
    return factor * (2.0 * (k_one * k_two)) / safe


def split(values):
    head = values.astype(BF16)
    tail = (values - head.astype(F32)).astype(BF16)
    return head, tail


def offset_of(digit):
    return lax.rem(jnp.where(digit < 2, 2 - digit, digit + 1), 4)


def kernel(
    right_ref,
    perm_ref,
    acc_ref,
    active_ref,
    local_ref,
    remote_ref,
    mult_ref,
    count_ref,
    low_ref,
    high_ref,
    corr_ref,
    resid_ref,
    keff,
    diag_acc,
    diagonal,
    step_ref,
    trans,
    cell_row,
    lo_ref,
    hot_lanes,
    hot_rows,
    table,
    fault_trans,
    turned,
    send_a,
    recv_a,
    send_b,
    recv_b,
    send_p,
    recv_p,
    face_x_out,
    face_x_in,
    face_y_out,
    face_y_in,
    ssem,
    rsem,
    face_ssem,
    face_rsem,
):
    gx = lax.axis_index("gx")
    gy = lax.axis_index("gy")
    px, pz = gx // 4, lax.rem(gx, 4)
    py, pc = gy // 2, lax.rem(gy, 2)

    def peer(slot):
        dx = offset_of(slot // 32)
        dz = offset_of(lax.rem(slot // 8, 4))
        dy = offset_of(lax.rem(slot // 2, 4))
        dc = 1 - lax.rem(slot, 2)
        return (
            lax.rem(px + dx, 4) * 4 + lax.rem(pz + dz, 4),
            lax.rem(py + dy, 4) * 2 + lax.rem(pc + dc, 2),
        )

    def mirror(slot):
        def turn(digit):
            inner = jnp.logical_and(digit > 0, digit < 3)
            return jnp.where(inner, 3 - digit, digit)

        return (
            turn(slot // 32) * 32
            + turn(lax.rem(slot // 8, 4)) * 8
            + turn(lax.rem(slot // 2, 4)) * 2
            + lax.rem(slot, 2)
        )

    barrier = pltpu.get_barrier_semaphore()

    def greet(slot, carry):
        pl.semaphore_signal(barrier, inc=1, device_id=peer(slot), device_id_type=MESH)
        return carry

    lax.fori_loop(0, PEERS - 1, greet, 0)

    lane = lax.broadcasted_iota(jnp.int32, (1, LANES), 1)

    def order(slot, carry):
        ox, oy = peer(slot)
        owner = ox * 8 + oy
        cell_row[pl.ds(slot, 1), :] = local_ref[pl.ds(owner, 1), :]
        send_a[slot, 0:1, :] = remote_ref[pl.ds(owner, 1), :].astype(F32)
        mult = mult_ref[pl.ds(owner, 1), :]
        send_a[slot, 2:3, :] = jnp.where(lane < count_ref[0, owner], mult, 0.0)
        return carry

    lax.fori_loop(0, PEERS, order, 0)

    keff[...] = jnp.where(active_ref[...] != 0, perm_ref[...], 0.0)
    diag_acc[...] = jnp.where(active_ref[...] != 0, acc_ref[...], 1.0)

    def index_rows(kind):
        cells = cell_row[...]
        low = ((cells >> 12) * 2 + ((cells >> 8) & 1)) * 8 + ((cells >> 9) & 7)
        for chunk in range(CHUNKS):
            base = chunk * 2 * PER + kind * PER
            lo_ref[base : base + PER, :] = low[chunk * PER : (chunk + 1) * PER]
        turned[...] = jnp.transpose(cells & 255)
        down = lax.broadcasted_iota(jnp.int32, (256, LANES), 0)
        across = lax.broadcasted_iota(jnp.int32, (LANES, LANES), 1)

        def one(slot, carry):
            place = (slot // PER) * 2 * PER + kind * PER + lax.rem(slot, PER)
            start = pl.multiple_of(place * LANES, LANES)
            high = jnp.broadcast_to(cell_row[pl.ds(slot, 1), :] & 255, (256, LANES))
            hot_lanes[:, pl.ds(start, LANES)] = jnp.where(high == down, 1.0, 0.0).astype(BF16)
            pick = jnp.full((8, LANES), slot, jnp.int32)
            column = jnp.concatenate(
                [
                    jnp.take_along_axis(
                        turned[8 * i : 8 * i + 8, :], pick, axis=1, mode="promise_in_bounds"
                    )
                    for i in range(16)
                ],
                axis=0,
            )
            hot_rows[pl.ds(start, LANES), 0:128] = jnp.where(column == across, 1.0, 0.0).astype(BF16)
            hot_rows[pl.ds(start, LANES), 128:256] = jnp.where(
                column == across + 128, 1.0, 0.0
            ).astype(BF16)
            return carry

        lax.fori_loop(0, PEERS, one, 0)

    def set_table(values):
        for a in range(4):
            for h in range(2):
                row = (a * 2 + h) * 8
                head, tail = split(values[a, :, h * 256 : h * 256 + 256])
                table[row : row + 8, :] = head.astype(F32)
                table[64 + row : 72 + row, :] = tail.astype(F32)

    def gather(first, count, write):
        down = lax.broadcasted_iota(jnp.int32, (64, LANES), 0)
        start = pl.multiple_of(first * LANES, LANES)
        rows = table[...].astype(BF16)
        found = jnp.dot(
            rows, hot_lanes[:, pl.ds(start, count * LANES)], preferred_element_type=F32
        )
        for i in range(count):
            block = found[0:64, i * LANES : (i + 1) * LANES] + found[64:128, i * LANES : (i + 1) * LANES]
            mask = down == jnp.broadcast_to(lo_ref[pl.ds(first + i, 1), :], (64, LANES))
            write(i, jnp.sum(jnp.where(mask, block, 0.0), axis=0, keepdims=True))

    def scatter(first, count, values, total):
        down = lax.broadcasted_iota(jnp.int32, (64, LANES), 0)
        zero = jnp.zeros((64, LANES), BF16)
        heads, tails = [], []
        for i in range(count):
            head, tail = split(values(i))
            mask = down == jnp.broadcast_to(lo_ref[pl.ds(first + i, 1), :], (64, LANES))
            heads.append(jnp.where(mask, jnp.broadcast_to(head, (64, LANES)), zero))
            tails.append(jnp.where(mask, jnp.broadcast_to(tail, (64, LANES)), zero))
        spread = jnp.concatenate(
            [jnp.concatenate(heads, axis=1), jnp.concatenate(tails, axis=1)], axis=0
        )
        start = pl.multiple_of(first * LANES, LANES)
        return total + jnp.dot(
            spread, hot_rows[pl.ds(start, count * LANES), :], preferred_element_type=F32
        )

    def send(phase, chunk, source, target):
        def one(i, carry):
            slot = chunk * PER + i
            back = mirror(slot)
            pltpu.make_async_remote_copy(
                src_ref=source.at[slot],
                dst_ref=target.at[back],
                send_sem=ssem.at[phase],
                recv_sem=rsem.at[phase, back // PER],
                device_id=peer(slot),
                device_id_type=MESH,
            ).start()
            return carry

        lax.fori_loop(0, jnp.where(chunk == CHUNKS - 1, PER - 1, PER), one, 0)

    def wait_chunk(phase, chunk, target):
        count = PER - 1 if chunk == CHUNKS - 1 else PER
        block = target.at[pl.ds(chunk * PER, count)]
        pltpu.make_async_copy(block, block, rsem.at[phase, chunk]).wait()

    def wait_sent(phase, source):
        block = source.at[pl.ds(0, PEERS - 1)]
        pltpu.make_async_copy(block, block, ssem.at[phase]).wait()

    def face_copies(phase):
        west = (lax.rem(gx + 15, 16), gy)
        east = (lax.rem(gx + 1, 16), gy)
        south = (gx, lax.rem(gy + 7, 8))
        north = (gx, lax.rem(gy + 1, 8))
        plan = (
            (face_x_out, face_x_in, 0, 1, west),
            (face_x_out, face_x_in, 1, 0, east),
            (face_y_out, face_y_in, 0, 1, south),
            (face_y_out, face_y_in, 1, 0, north),
        )
        copies = []
        for number, (out, into, side, other, device) in enumerate(plan):
            copies.append(
                pltpu.make_async_remote_copy(
                    src_ref=out.at[phase, side],
                    dst_ref=into.at[phase, other],
                    send_sem=face_ssem.at[phase, number],
                    recv_sem=face_rsem.at[phase, number],
                    device_id=device,
                    device_id_type=MESH,
                )
            )
        return copies

    def send_faces(phase, values):
        face_x_out[phase, 0] = values[0]
        face_x_out[phase, 1] = values[3]
        for a in range(4):
            face_y_out[phase, 0, a : a + 1, :] = values[a, 0:1, :]
            face_y_out[phase, 1, a : a + 1, :] = values[a, 7:8, :]
        for copy in face_copies(phase):
            copy.start()

    def beside(values, phase, a):
        plane = values[a]
        east = values[a + 1] if a < 3 else face_x_in[phase, 1]
        west = values[a - 1] if a > 0 else face_x_in[phase, 0]
        north = jnp.concatenate([plane[1:8], face_y_in[phase, 1, a : a + 1, :]], axis=0)
        south = jnp.concatenate([face_y_in[phase, 0, a : a + 1, :], plane[0:7]], axis=0)
        above = pltpu.roll(plane, 511, 1)
        below = pltpu.roll(plane, 1, 1)
        return plane, (east, west, north, south, above, below)

    index_rows(0)
    set_table(keff)

    for chunk in range(CHUNKS):

        def put_k(i, row, chunk=chunk):
            send_a[chunk * PER + i, 1:2, :] = row

        gather(chunk * 2 * PER, PER, put_k)

    pl.semaphore_wait(barrier, PEERS - 1)

    for chunk in range(CHUNKS):
        send(0, chunk, send_a, recv_a)
    send_faces(0, keff)
    recv_a[PEERS - 1] = send_a[PEERS - 1]
    for chunk in range(CHUNKS):
        wait_chunk(0, chunk, recv_a)
        for i in range(PER):
            slot = chunk * PER + i
            cell_row[slot : slot + 1, :] = recv_a[slot, 0:1, :].astype(jnp.int32)
    index_rows(1)

    for chunk in range(CHUNKS):

        def put_k(i, row, chunk=chunk):
            send_b[chunk * PER + i, 0:1, :] = row

        gather(chunk * 2 * PER + PER, PER, put_k)
        send(1, chunk, send_b, recv_b)
    recv_b[PEERS - 1] = send_b[PEERS - 1]
    for copy in face_copies(0):
        copy.wait_recv()

    at_x = (gx > 0, gx < 15)
    at_y = (gy > 0, gy < 7)
    for side in range(2):
        face_x_in[0, side] = jnp.where(at_x[side], face_x_in[0, side], 0.0)
        face_y_in[0, side] = jnp.where(at_y[side], face_y_in[0, side], 0.0)
    layer = lax.broadcasted_iota(jnp.int32, (8, 512), 1)
    for a in range(4):
        plane, others = beside(keff, 0, a)
        amount = diag_acc[a]
        for side in range(6):
            other = others[side]
            if side == 4:
                other = jnp.where(layer == 511, 0.0, other)
            if side == 5:
                other = jnp.where(layer == 0, 0.0, other)
            one = harmonic(plane, other, 0.8 if side >= 4 else 1.0)
            trans[side, a] = one
            amount = amount + one
        diagonal[a] = amount

    total = jnp.zeros((128, 256), F32)
    for chunk in range(CHUNKS):
        first = chunk * 2 * PER

        def asked(i, chunk=chunk, first=first):
            slot = chunk * PER + i
            value = (
                harmonic(recv_a[slot, 1:2, :], send_b[slot, 0:1, :], 1.0) * recv_a[slot, 2:3, :]
            )
            fault_trans[first + PER + i : first + PER + i + 1, :] = value
            return value

        total = scatter(first + PER, PER, asked, total)
    for chunk in range(CHUNKS):
        wait_chunk(1, chunk, recv_b)
        first = chunk * 2 * PER

        def owned(i, chunk=chunk, first=first):
            slot = chunk * PER + i
            value = (
                harmonic(send_a[slot, 1:2, :], recv_b[slot, 0:1, :], 1.0) * send_a[slot, 2:3, :]
            )
            fault_trans[first + i : first + i + 1, :] = value
            return value

        total = scatter(first, PER, owned, total)

    def place(total, a):
        halves = [
            total[(a * 2 + h) * 8 : (a * 2 + h) * 8 + 8, :]
            + total[64 + (a * 2 + h) * 8 : 64 + (a * 2 + h) * 8 + 8, :]
            for h in range(2)
        ]
        return jnp.concatenate(halves, axis=1)

    low = jnp.full((8, 512), low_ref[0], F32)
    high = jnp.full((8, 512), high_ref[0], F32)
    theta = (high + low) / 2.0
    delta = (high - low) / 2.0
    sigma = theta / delta
    for a in range(4):
        diagonal[a] = diagonal[a] + place(total, a)
        resid_ref[a] = right_ref[a]
        step_ref[a] = right_ref[a] / diagonal[a] / theta
        corr_ref[a] = jnp.zeros((8, 512), F32)

    def iteration(count, rho):
        phase = count + 2
        face_phase = count + 1
        send_faces(face_phase, step_ref)
        set_table(step_ref)
        source, target = send_p.at[count], recv_p.at[count]

        def ask(chunk, carry):
            for kind in range(2):

                def put_p(i, row, kind=kind):
                    source[chunk * PER + i, kind : kind + 1, :] = row

                gather(chunk * 2 * PER + kind * PER, PER, put_p)
            send(phase, chunk, source, target)
            return carry

        lax.fori_loop(0, CHUNKS, ask, 0)
        target[PEERS - 1] = source[PEERS - 1]
        total = jnp.zeros((128, 256), F32)
        for chunk in range(CHUNKS):
            wait_chunk(phase, chunk, target)
            first = chunk * 2 * PER

            def flux(i, chunk=chunk, first=first):
                slot, kind = chunk * PER + i % PER, i // PER
                return fault_trans[first + i : first + i + 1, :] * (
                    source[slot, kind : kind + 1, :] - target[slot, 1 - kind : 2 - kind, :]
                )

            total = scatter(first, 2 * PER, flux, total)
        for copy in face_copies(face_phase):
            copy.wait_recv()
        rho_new = 1.0 / (2.0 * sigma - rho)
        news = []
        for a in range(4):
            plane, others = beside(step_ref, face_phase, a)
            result = diag_acc[a] * plane
            for side in range(6):
                result = result + trans[side, a] * (plane - others[side])
            corr_ref[a] = corr_ref[a] + plane
            resid = resid_ref[a] - (result + place(total, a))
            resid_ref[a] = resid
            news.append(rho_new * rho * plane + 2.0 * rho_new / delta * (resid / diagonal[a]))
        for a in range(4):
            step_ref[a] = news[a]
        wait_sent(phase, source)
        for copy in face_copies(face_phase):
            copy.wait_send()
        return rho_new

    lax.fori_loop(0, ITERS, iteration, 1.0 / sigma)
    wait_sent(0, send_a)
    wait_sent(1, send_b)
    for copy in face_copies(0):
        copy.wait_send()


def on_device(
    right_side,
    permeability,
    accumulation,
    active,
    fault_local,
    fault_remote,
    fault_count,
    fault_mult,
    low_bound,
    high_bound,
):
    shape = right_side.shape
    vmem = pl.BlockSpec(memory_space=pltpu.VMEM)
    smem = pl.BlockSpec(memory_space=pltpu.SMEM)
    rows = 2 * PEERS
    cells = pltpu.VMEM(shape, F32)
    return tuple(
        pl.pallas_call(
            kernel,
            out_shape=[jax.ShapeDtypeStruct(shape, F32)] * 2,
            in_specs=[vmem] * 7 + [smem] * 3,
            out_specs=[vmem] * 2,
            scratch_shapes=[
                cells,
                cells,
                cells,
                cells,
                pltpu.VMEM((6,) + shape, F32),
                pltpu.VMEM((PEERS, LANES), jnp.int32),
                pltpu.VMEM((rows, LANES), jnp.int32),
                pltpu.VMEM((256, rows * LANES), BF16),
                pltpu.VMEM((rows * LANES, 256), BF16),
                pltpu.VMEM((128, 256), F32),
                pltpu.VMEM((rows, LANES), F32),
                pltpu.VMEM((LANES, LANES), jnp.int32),
                pltpu.VMEM((PEERS, 4, LANES), F32),
                pltpu.VMEM((PEERS, 4, LANES), F32),
                pltpu.VMEM((PEERS, 1, LANES), F32),
                pltpu.VMEM((PEERS, 1, LANES), F32),
                pltpu.VMEM((ITERS, PEERS, 2, LANES), F32),
                pltpu.VMEM((ITERS, PEERS, 2, LANES), F32),
                pltpu.VMEM((ITERS + 1, 2, 8, 512), F32),
                pltpu.VMEM((ITERS + 1, 2, 8, 512), F32),
                pltpu.VMEM((ITERS + 1, 2, 4, 512), F32),
                pltpu.VMEM((ITERS + 1, 2, 4, 512), F32),
                pltpu.SemaphoreType.DMA((ITERS + 2,)),
                pltpu.SemaphoreType.DMA((ITERS + 2, CHUNKS)),
                pltpu.SemaphoreType.DMA((ITERS + 1, 4)),
                pltpu.SemaphoreType.DMA((ITERS + 1, 4)),
            ],
            compiler_params=pltpu.CompilerParams(
                collective_id=0, has_side_effects=True, vmem_limit_bytes=56 * 2**20
            ),
        )(
            right_side,
            permeability,
            accumulation,
            active,
            fault_local.reshape(PEERS, LANES),
            fault_remote.reshape(PEERS, LANES),
            fault_mult.reshape(PEERS, LANES),
            fault_count,
            low_bound,
            high_bound,
        )
    )


def solution(mesh):
    in_specs = (
        P("gx", "gy", None),
        P("gx", "gy", None),
        P("gx", "gy", None),
        P("gx", "gy", None),
        P(("gx", "gy"), None, None),
        P(("gx", "gy"), None, None),
        P(("gx", "gy"), None),
        P(("gx", "gy"), None, None),
        P(),
        P(),
    )
    out_specs = (P("gx", "gy", None), P("gx", "gy", None))
    return jax.shard_map(
        on_device, mesh=mesh, in_specs=in_specs, out_specs=out_specs, check_vma=False
    )
```

time: 2110 us -> 120 us (0.06)
  local copies, waits for them, and re-layouts: 1260 us -> 2.14 us
  other arithmetic: 704 us -> 0 us
  starting transfers between devices: 128 us -> 0 us
  Pallas kernels: 0 us -> 116 us
    gather x10 -> x0, local copies, waits for them, and re-layouts: 1260 us -> none  [the longest x3 481 us: on_device(): asked_values = flat[requests]]
    scatter-add x8 -> x0, other arithmetic: 696 us -> none  [the longest x6 522 us: on_device(): extra = jnp.zeros(cells, jnp.float32).at[local_list].add(own_flux.reshape...]
    pallas_call x0 -> x1, Pallas kernels: none -> 116 us  [on_device(): pl.pallas_call(kernel, out_shape=[jax.ShapeDtypeStruct(shape, F32)] * 2,...]
    all_to_all x10 -> x0, starting transfers between devices: 86.6 us -> none  [the longest x9 75.1 us: fault_move(): lax.all_to_all(values, ('gx', 'gy'), split_axis=1, concat_axis=1, tiled=T...]
    ppermute x16 -> x0, starting transfers between devices: 41.2 us -> none  [the longest x8 25.2 us: padded_2(): lax.ppermute(tail, axis, [(i, (i + 1) % count) for i in range(ends)])]
  transfers between devices with their start and end apart: 26 -> 0, of which waited for: 4 -> 0; matrix products, arithmetic and copies ran while one was open for 88% -> 0% of each run, Pallas kernels for 0% -> 0%
where the time goes in v1:
time: 120 us
  Pallas kernels  116 us (97%)
  local copies, waits for them, and re-layouts  2.14 us (2%)
  between operations  1.94 us (2%)
    pallas_call x1, Pallas kernels, on_device(): pl.pallas_call(kernel, out_shape=[jax.ShapeDtypeStruct(shape, F32)] * 2,...  116 us

profile of v1, /device:TPU:1, one launch (start us, length us, event | category | flops | bytes accessed | tf_op | source)
XLA Modules:
  0.0 120.2 jit_solution(6959134942405587226)
XLA Ops:
  1.9 116.1 %shard_map.113 = (f32[4,8,512]{2,1,0:T(8,128)}, f32[4,8,512]{2,1,0:T(8,128)}) custom-call(f32[4,8,512]{2,1,0:T(8,128)} %right_ref.1, f32[4,8,512]{2,1,0:T(8,128)} %perm_ref.1, f32[4,8,512]{2,1,0:T(8,128)} %acc_ref.1, s32[4,8,512]{2,1,0:T(8,128)} %active_ref.1, s32[128,128]{1,0:T(8,128)} %bitcast.3, s32[128,128]{1,0:T(8,128)} %bitcast.4, f32[128,128]{1,0:T(8,128)} %bitcast.5, ...), custom_call_target="tpu_custom_call" | custom-call | tf_op jit(solution)/shard_map/pallas_call | solution.py:442
  118.0 0.0 copy-start
  118.0 1.5 %copy.16 = f32[4,8,512]{2,1,0:T(8,128)} copy(f32[4,8,512]{2,1,0:T(8,128)} %get-tuple-element.4) | data formatting | bytes 131072
  119.5 0.0 copy-done
  119.5 0.6 copy.17
Async XLA Ops:
  118.0 1.5 %copy-start = (f32[4,8,512]{2,1,0:T(8,128)S(1)}, f32[4,8,512]{2,1,0:T(8,128)}, u32[]{:S(2)}) copy-start(f32[4,8,512]{2,1,0:T(8,128)} %get-tuple-element.5) | copy-start | bytes 196612

commit v2 on v1

--- a/solution.py
+++ b/solution.py
@@ -29,8 +29,26 @@
     return head, tail
 
 
-def offset_of(digit):
-    return lax.rem(jnp.where(digit < 2, 2 - digit, digit + 1), 4)
+def slot_plan():
+    def hops(offset):
+        return sum(min(d, 4 - d) for d in offset[:3])
+
+    def opposite(offset):
+        return tuple(-d % 4 for d in offset[:3]) + (offset[3],)
+
+    offsets = [(x, z, y, c) for x in range(4) for z in range(4) for y in range(4) for c in range(2)]
+
+    def rank(offset):
+        pair = min(offset[:3], opposite(offset)[:3])
+        alone = offset[:3] == opposite(offset)[:3]
+        first = alone if hops(offset) == 2 else not alone
+        return (-hops(offset), first, pair, offset[:3], 1 - offset[3])
+
+    offsets.sort(key=rank)
+    return offsets, [offsets.index(opposite(offset)) for offset in offsets]
+
+
+OFFSETS, MIRROR = slot_plan()
 
 
 def kernel(
@@ -58,6 +76,9 @@
     table,
     fault_trans,
     turned,
+    grid_part,
+    send_i,
+    recv_i,
     send_a,
     recv_a,
     send_b,
@@ -75,87 +96,77 @@
 ):
     gx = lax.axis_index("gx")
     gy = lax.axis_index("gy")
-    px, pz = gx // 4, lax.rem(gx, 4)
-    py, pc = gy // 2, lax.rem(gy, 2)
+    at_x = [lax.rem(gx // 4 + d, 4) * 4 for d in range(4)]
+    at_z = [lax.rem(lax.rem(gx, 4) + d, 4) for d in range(4)]
+    at_y = [lax.rem(gy // 2 + d, 4) * 2 for d in range(4)]
+    at_c = [lax.rem(lax.rem(gy, 2) + d, 2) for d in range(2)]
 
     def peer(slot):
-        dx = offset_of(slot // 32)
-        dz = offset_of(lax.rem(slot // 8, 4))
-        dy = offset_of(lax.rem(slot // 2, 4))
-        dc = 1 - lax.rem(slot, 2)
-        return (
-            lax.rem(px + dx, 4) * 4 + lax.rem(pz + dz, 4),
-            lax.rem(py + dy, 4) * 2 + lax.rem(pc + dc, 2),
-        )
-
-    def mirror(slot):
-        def turn(digit):
-            inner = jnp.logical_and(digit > 0, digit < 3)
-            return jnp.where(inner, 3 - digit, digit)
-
-        return (
-            turn(slot // 32) * 32
-            + turn(lax.rem(slot // 8, 4)) * 8
-            + turn(lax.rem(slot // 2, 4)) * 2
-            + lax.rem(slot, 2)
-        )
+        dx, dz, dy, dc = OFFSETS[slot]
+        return (at_x[dx] + at_z[dz], at_y[dy] + at_c[dc])
 
     barrier = pltpu.get_barrier_semaphore()
 
-    def greet(slot, carry):
+    for slot in range(PEERS - 1):
         pl.semaphore_signal(barrier, inc=1, device_id=peer(slot), device_id_type=MESH)
-        return carry
-
-    lax.fori_loop(0, PEERS - 1, greet, 0)
 
     lane = lax.broadcasted_iota(jnp.int32, (1, LANES), 1)
-
-    def order(slot, carry):
+    for slot in range(PEERS):
         ox, oy = peer(slot)
         owner = ox * 8 + oy
-        cell_row[pl.ds(slot, 1), :] = local_ref[pl.ds(owner, 1), :]
-        send_a[slot, 0:1, :] = remote_ref[pl.ds(owner, 1), :].astype(F32)
+        cell_row[slot : slot + 1, :] = local_ref[pl.ds(owner, 1), :]
+        send_i[slot, 0:1, :] = remote_ref[pl.ds(owner, 1), :]
         mult = mult_ref[pl.ds(owner, 1), :]
-        send_a[slot, 2:3, :] = jnp.where(lane < count_ref[0, owner], mult, 0.0)
-        return carry
-
-    lax.fori_loop(0, PEERS, order, 0)
+        send_a[slot, 1:2, :] = jnp.where(lane < count_ref[0, owner], mult, 0.0)
 
     keff[...] = jnp.where(active_ref[...] != 0, perm_ref[...], 0.0)
     diag_acc[...] = jnp.where(active_ref[...] != 0, acc_ref[...], 1.0)
 
+    down = lax.broadcasted_iota(jnp.int32, (256, LANES), 0)
+    across = lax.broadcasted_iota(jnp.int32, (LANES, LANES), 1)
+
+    def index_lanes(kind, chunk):
+        cells = cell_row[chunk * PER : (chunk + 1) * PER, :]
+        base = chunk * 2 * PER + kind * PER
+        lo_ref[base : base + PER, :] = (
+            ((cells >> 12) * 2 + ((cells >> 8) & 1)) * 8 + ((cells >> 9) & 7)
+        )
+
+        def some(step, carry):
+            for i in range(8):
+                row = chunk * PER + step * 8 + i
+                start = pl.multiple_of((base + step * 8 + i) * LANES, LANES)
+                high = jnp.broadcast_to(cell_row[pl.ds(row, 1), :] & 255, (256, LANES))
+                hot_lanes[:, pl.ds(start, LANES)] = jnp.where(high == down, 1.0, 0.0).astype(BF16)
+            return carry
+
+        lax.fori_loop(0, PER // 8, some, 0)
+
     def index_rows(kind):
-        cells = cell_row[...]
-        low = ((cells >> 12) * 2 + ((cells >> 8) & 1)) * 8 + ((cells >> 9) & 7)
-        for chunk in range(CHUNKS):
-            base = chunk * 2 * PER + kind * PER
-            lo_ref[base : base + PER, :] = low[chunk * PER : (chunk + 1) * PER]
-        turned[...] = jnp.transpose(cells & 255)
-        down = lax.broadcasted_iota(jnp.int32, (256, LANES), 0)
-        across = lax.broadcasted_iota(jnp.int32, (LANES, LANES), 1)
-
-        def one(slot, carry):
-            place = (slot // PER) * 2 * PER + kind * PER + lax.rem(slot, PER)
-            start = pl.multiple_of(place * LANES, LANES)
-            high = jnp.broadcast_to(cell_row[pl.ds(slot, 1), :] & 255, (256, LANES))
-            hot_lanes[:, pl.ds(start, LANES)] = jnp.where(high == down, 1.0, 0.0).astype(BF16)
-            pick = jnp.full((8, LANES), slot, jnp.int32)
-            column = jnp.concatenate(
-                [
-                    jnp.take_along_axis(
-                        turned[8 * i : 8 * i + 8, :], pick, axis=1, mode="promise_in_bounds"
-                    )
-                    for i in range(16)
-                ],
-                axis=0,
-            )
-            hot_rows[pl.ds(start, LANES), 0:128] = jnp.where(column == across, 1.0, 0.0).astype(BF16)
-            hot_rows[pl.ds(start, LANES), 128:256] = jnp.where(
-                column == across + 128, 1.0, 0.0
-            ).astype(BF16)
+        turned[...] = jnp.transpose(cell_row[...] & 255)
+
+        def some(step, carry):
+            for i in range(4):
+                slot = step * 4 + i
+                pick = jnp.full((8, LANES), slot, jnp.int32)
+                column = jnp.concatenate(
+                    [
+                        jnp.take_along_axis(
+                            turned[8 * j : 8 * j + 8, :], pick, axis=1, mode="promise_in_bounds"
+                        )
+                        for j in range(16)
+                    ],
+                    axis=0,
+                )
+                place = (slot // PER) * 2 * PER + kind * PER + lax.rem(slot, PER)
+                start = pl.multiple_of(place * LANES, LANES)
+                for half in range(2):
+                    hot_rows[pl.ds(start, LANES), half * 128 : half * 128 + 128] = jnp.where(
+                        column == across + half * 128, 1.0, 0.0
+                    ).astype(BF16)
             return carry
 
-        lax.fori_loop(0, PEERS, one, 0)
+        lax.fori_loop(0, PEERS // 4, some, 0)
 
     def set_table(values):
         for a in range(4):
@@ -195,20 +206,17 @@
         )
 
     def send(phase, chunk, source, target):
-        def one(i, carry):
-            slot = chunk * PER + i
-            back = mirror(slot)
-            pltpu.make_async_remote_copy(
-                src_ref=source.at[slot],
-                dst_ref=target.at[back],
-                send_sem=ssem.at[phase],
-                recv_sem=rsem.at[phase, back // PER],
-                device_id=peer(slot),
-                device_id_type=MESH,
-            ).start()
-            return carry
-
-        lax.fori_loop(0, jnp.where(chunk == CHUNKS - 1, PER - 1, PER), one, 0)
+        for slot in range(chunk * PER, (chunk + 1) * PER):
+            if slot < PEERS - 1:
+                back = MIRROR[slot]
+                pltpu.make_async_remote_copy(
+                    src_ref=source.at[slot],
+                    dst_ref=target.at[back],
+                    send_sem=ssem.at[phase],
+                    recv_sem=rsem.at[phase, back // PER],
+                    device_id=peer(slot),
+                    device_id_type=MESH,
+                ).start()
 
     def wait_chunk(phase, chunk, target):
         count = PER - 1 if chunk == CHUNKS - 1 else PER
@@ -263,45 +271,48 @@
         below = pltpu.roll(plane, 1, 1)
         return plane, (east, west, north, south, above, below)
 
+    set_table(keff)
+    for chunk in range(CHUNKS):
+
+        def put_k(i, row, chunk=chunk):
+            send_a[chunk * PER + i, 0:1, :] = row
+
+        index_lanes(0, chunk)
+        gather(chunk * 2 * PER, PER, put_k)
     index_rows(0)
-    set_table(keff)
+
+    pl.semaphore_wait(barrier, PEERS - 1)
 
     for chunk in range(CHUNKS):
-
-        def put_k(i, row, chunk=chunk):
-            send_a[chunk * PER + i, 1:2, :] = row
-
-        gather(chunk * 2 * PER, PER, put_k)
-
-    pl.semaphore_wait(barrier, PEERS - 1)
-
+        send(0, chunk, send_i, recv_i)
+    send_faces(0, keff)
     for chunk in range(CHUNKS):
-        send(0, chunk, send_a, recv_a)
-    send_faces(0, keff)
+        send(1, chunk, send_a, recv_a)
+    recv_i[PEERS - 1] = send_i[PEERS - 1]
     recv_a[PEERS - 1] = send_a[PEERS - 1]
+
     for chunk in range(CHUNKS):
-        wait_chunk(0, chunk, recv_a)
+        wait_chunk(0, chunk, recv_i)
         for i in range(PER):
             slot = chunk * PER + i
-            cell_row[slot : slot + 1, :] = recv_a[slot, 0:1, :].astype(jnp.int32)
-    index_rows(1)
-
-    for chunk in range(CHUNKS):
+            cell_row[slot : slot + 1, :] = recv_i[slot, 0:1, :]
+        index_lanes(1, chunk)
 
         def put_k(i, row, chunk=chunk):
             send_b[chunk * PER + i, 0:1, :] = row
 
         gather(chunk * 2 * PER + PER, PER, put_k)
-        send(1, chunk, send_b, recv_b)
+        send(2, chunk, send_b, recv_b)
     recv_b[PEERS - 1] = send_b[PEERS - 1]
+    index_rows(1)
     for copy in face_copies(0):
         copy.wait_recv()
 
-    at_x = (gx > 0, gx < 15)
-    at_y = (gy > 0, gy < 7)
+    inside_x = (gx > 0, gx < 15)
+    inside_y = (gy > 0, gy < 7)
     for side in range(2):
-        face_x_in[0, side] = jnp.where(at_x[side], face_x_in[0, side], 0.0)
-        face_y_in[0, side] = jnp.where(at_y[side], face_y_in[0, side], 0.0)
+        face_x_in[0, side] = jnp.where(inside_x[side], face_x_in[0, side], 0.0)
+        face_y_in[0, side] = jnp.where(inside_y[side], face_y_in[0, side], 0.0)
     layer = lax.broadcasted_iota(jnp.int32, (8, 512), 1)
     for a in range(4):
         plane, others = beside(keff, 0, a)
@@ -319,25 +330,26 @@
 
     total = jnp.zeros((128, 256), F32)
     for chunk in range(CHUNKS):
+        wait_chunk(1, chunk, recv_a)
         first = chunk * 2 * PER
 
         def asked(i, chunk=chunk, first=first):
             slot = chunk * PER + i
             value = (
-                harmonic(recv_a[slot, 1:2, :], send_b[slot, 0:1, :], 1.0) * recv_a[slot, 2:3, :]
+                harmonic(recv_a[slot, 0:1, :], send_b[slot, 0:1, :], 1.0) * recv_a[slot, 1:2, :]
             )
             fault_trans[first + PER + i : first + PER + i + 1, :] = value
             return value
 
         total = scatter(first + PER, PER, asked, total)
     for chunk in range(CHUNKS):
-        wait_chunk(1, chunk, recv_b)
+        wait_chunk(2, chunk, recv_b)
         first = chunk * 2 * PER
 
         def owned(i, chunk=chunk, first=first):
             slot = chunk * PER + i
             value = (
-                harmonic(send_a[slot, 1:2, :], recv_b[slot, 0:1, :], 1.0) * send_a[slot, 2:3, :]
+                harmonic(send_a[slot, 0:1, :], recv_b[slot, 0:1, :], 1.0) * send_a[slot, 1:2, :]
             )
             fault_trans[first + i : first + i + 1, :] = value
             return value
@@ -352,8 +364,8 @@
         ]
         return jnp.concatenate(halves, axis=1)
 
-    low = jnp.full((8, 512), low_ref[0], F32)
-    high = jnp.full((8, 512), high_ref[0], F32)
+    low = jnp.broadcast_to(low_ref[...], (8, 512))
+    high = jnp.broadcast_to(high_ref[...], (8, 512))
     theta = (high + low) / 2.0
     delta = (high - low) / 2.0
     sigma = theta / delta
@@ -364,61 +376,55 @@
         corr_ref[a] = jnp.zeros((8, 512), F32)
 
     def iteration(count, rho):
-        phase = count + 2
+        phase = count + 3
         face_phase = count + 1
         send_faces(face_phase, step_ref)
         set_table(step_ref)
         source, target = send_p.at[count], recv_p.at[count]
-
-        def ask(chunk, carry):
+        for chunk in range(CHUNKS):
             for kind in range(2):
 
-                def put_p(i, row, kind=kind):
+                def put_p(i, row, chunk=chunk, kind=kind):
                     source[chunk * PER + i, kind : kind + 1, :] = row
 
                 gather(chunk * 2 * PER + kind * PER, PER, put_p)
             send(phase, chunk, source, target)
-            return carry
-
-        lax.fori_loop(0, CHUNKS, ask, 0)
         target[PEERS - 1] = source[PEERS - 1]
-        total = jnp.zeros((128, 256), F32)
-        for chunk in range(CHUNKS):
-            wait_chunk(phase, chunk, target)
-            first = chunk * 2 * PER
-
-            def flux(i, chunk=chunk, first=first):
-                slot, kind = chunk * PER + i % PER, i // PER
-                return fault_trans[first + i : first + i + 1, :] * (
-                    source[slot, kind : kind + 1, :] - target[slot, 1 - kind : 2 - kind, :]
-                )
-
-            total = scatter(first, 2 * PER, flux, total)
         for copy in face_copies(face_phase):
             copy.wait_recv()
-        rho_new = 1.0 / (2.0 * sigma - rho)
-        news = []
         for a in range(4):
             plane, others = beside(step_ref, face_phase, a)
             result = diag_acc[a] * plane
             for side in range(6):
                 result = result + trans[side, a] * (plane - others[side])
             corr_ref[a] = corr_ref[a] + plane
-            resid = resid_ref[a] - (result + place(total, a))
+            grid_part[a] = result
+        total = jnp.zeros((128, 256), F32)
+        for chunk in range(CHUNKS):
+            wait_chunk(phase, chunk, target)
+            first = chunk * 2 * PER
+
+            def flux(i, chunk=chunk, first=first):
+                slot, kind = chunk * PER + i % PER, i // PER
+                return fault_trans[first + i : first + i + 1, :] * (
+                    source[slot, kind : kind + 1, :] - target[slot, 1 - kind : 2 - kind, :]
+                )
+
+            total = scatter(first, 2 * PER, flux, total)
+        rho_new = 1.0 / (2.0 * sigma - rho)
+        for a in range(4):
+            resid = resid_ref[a] - (grid_part[a] + place(total, a))
             resid_ref[a] = resid
-            news.append(rho_new * rho * plane + 2.0 * rho_new / delta * (resid / diagonal[a]))
-        for a in range(4):
-            step_ref[a] = news[a]
+            step_ref[a] = rho_new * rho * step_ref[a] + 2.0 * rho_new / delta * (resid / diagonal[a])
+        return rho_new
+
+    lax.fori_loop(0, ITERS, iteration, 1.0 / sigma)
+    sent = [send_i, send_a, send_b] + [send_p.at[count] for count in range(ITERS)]
+    for phase, source in enumerate(sent):
         wait_sent(phase, source)
-        for copy in face_copies(face_phase):
+    for phase in range(ITERS + 1):
+        for copy in face_copies(phase):
             copy.wait_send()
-        return rho_new
-
-    lax.fori_loop(0, ITERS, iteration, 1.0 / sigma)
-    wait_sent(0, send_a)
-    wait_sent(1, send_b)
-    for copy in face_copies(0):
-        copy.wait_send()
 
 
 def on_device(
@@ -442,7 +448,7 @@
         pl.pallas_call(
             kernel,
             out_shape=[jax.ShapeDtypeStruct(shape, F32)] * 2,
-            in_specs=[vmem] * 7 + [smem] * 3,
+            in_specs=[vmem] * 7 + [smem] + [vmem] * 2,
             out_specs=[vmem] * 2,
             scratch_shapes=[
                 cells,
@@ -457,8 +463,11 @@
                 pltpu.VMEM((128, 256), F32),
                 pltpu.VMEM((rows, LANES), F32),
                 pltpu.VMEM((LANES, LANES), jnp.int32),
-                pltpu.VMEM((PEERS, 4, LANES), F32),
-                pltpu.VMEM((PEERS, 4, LANES), F32),
+                cells,
+                pltpu.VMEM((PEERS, 1, LANES), jnp.int32),
+                pltpu.VMEM((PEERS, 1, LANES), jnp.int32),
+                pltpu.VMEM((PEERS, 2, LANES), F32),
+                pltpu.VMEM((PEERS, 2, LANES), F32),
                 pltpu.VMEM((PEERS, 1, LANES), F32),
                 pltpu.VMEM((PEERS, 1, LANES), F32),
                 pltpu.VMEM((ITERS, PEERS, 2, LANES), F32),
@@ -467,8 +476,8 @@
                 pltpu.VMEM((ITERS + 1, 2, 8, 512), F32),
                 pltpu.VMEM((ITERS + 1, 2, 4, 512), F32),
                 pltpu.VMEM((ITERS + 1, 2, 4, 512), F32),
-                pltpu.SemaphoreType.DMA((ITERS + 2,)),
-                pltpu.SemaphoreType.DMA((ITERS + 2, CHUNKS)),
+                pltpu.SemaphoreType.DMA((ITERS + 3,)),
+                pltpu.SemaphoreType.DMA((ITERS + 3, CHUNKS)),
                 pltpu.SemaphoreType.DMA((ITERS + 1, 4)),
                 pltpu.SemaphoreType.DMA((ITERS + 1, 4)),
             ],
@@ -484,8 +493,8 @@
             fault_remote.reshape(PEERS, LANES),
             fault_mult.reshape(PEERS, LANES),
             fault_count,
-            low_bound,
-            high_bound,
+            low_bound.reshape(1, 1),
+            high_bound.reshape(1, 1),
         )
     )
 

time: 120 us -> 82.9 us (0.69)
  Pallas kernels: 116 us -> 78.6 us
    pallas_call x1, Pallas kernels: 116 us -> 78.6 us  [on_device(): pl.pallas_call(kernel, out_shape=[jax.ShapeDtypeStruct(shape, F32)] * 2,...]
where the time goes in v2:
time: 82.9 us; the launch traced here: 82.7 us
  Pallas kernels  78.6 us (95%)
  local copies, waits for them, and re-layouts  2.14 us (3%)
  between operations  1.94 us (2%)
    pallas_call x1, Pallas kernels, on_device(): pl.pallas_call(kernel, out_shape=[jax.ShapeDtypeStruct(shape, F32)] * 2,...  78.6 us
    unnamed x4, local copies, waits for them, and re-layouts  2.14 us

profile of v2, /device:TPU:1, one launch (start us, length us, event | category | flops | bytes accessed | tf_op | source)
XLA Modules:
  0.0 82.7 jit_solution(5583421338608582078)
XLA Ops:
  1.9 78.6 %shard_map.113 = (f32[4,8,512]{2,1,0:T(8,128)}, f32[4,8,512]{2,1,0:T(8,128)}) custom-call(f32[4,8,512]{2,1,0:T(8,128)} %right_ref.1, f32[4,8,512]{2,1,0:T(8,128)} %perm_ref.1, f32[4,8,512]{2,1,0:T(8,128)} %acc_ref.1, s32[4,8,512]{2,1,0:T(8,128)} %active_ref.1, s32[128,128]{1,0:T(8,128)} %bitcast.7, s32[128,128]{1,0:T(8,128)} %bitcast.8, f32[128,128]{1,0:T(8,128)} %bitcast.9, ...), custom_call_target="tpu_custom_call" | custom-call | tf_op jit(solution)/shard_map/pallas_call | solution.py:448
  80.5 0.0 copy-start
  80.6 1.5 %copy.16 = f32[4,8,512]{2,1,0:T(8,128)} copy(f32[4,8,512]{2,1,0:T(8,128)} %get-tuple-element.4) | data formatting | bytes 131072
  82.1 0.0 copy-done
  82.1 0.6 copy.17
Async XLA Ops:
  80.5 1.5 %copy-start = (f32[4,8,512]{2,1,0:T(8,128)S(1)}, f32[4,8,512]{2,1,0:T(8,128)}, u32[]{:S(2)}) copy-start(f32[4,8,512]{2,1,0:T(8,128)} %get-tuple-element.5) | copy-start | bytes 196612

commit v3 on v2

--- a/solution.py
+++ b/solution.py
@@ -31,21 +31,12 @@
 
 def slot_plan():
     def hops(offset):
-        return sum(min(d, 4 - d) for d in offset[:3])
-
-    def opposite(offset):
-        return tuple(-d % 4 for d in offset[:3]) + (offset[3],)
-
-    offsets = [(x, z, y, c) for x in range(4) for z in range(4) for y in range(4) for c in range(2)]
-
-    def rank(offset):
-        pair = min(offset[:3], opposite(offset)[:3])
-        alone = offset[:3] == opposite(offset)[:3]
-        first = alone if hops(offset) == 2 else not alone
-        return (-hops(offset), first, pair, offset[:3], 1 - offset[3])
-
-    offsets.sort(key=rank)
-    return offsets, [offsets.index(opposite(offset)) for offset in offsets]
+        return sum(min(d, 4 - d) for d in offset[:2])
+
+    offsets = [(z, y, c) for z in range(4) for y in range(4) for c in range(2)]
+    offsets.sort(key=lambda offset: (-hops(offset), offset[0], offset[1], 1 - offset[2]))
+    mirror = [offsets.index((-z % 4, -y % 4, c)) for z, y, c in offsets]
+    return offsets, mirror
 
 
 OFFSETS, MIRROR = slot_plan()
@@ -77,8 +68,6 @@
     fault_trans,
     turned,
     grid_part,
-    send_i,
-    recv_i,
     send_a,
     recv_a,
     send_b,
@@ -96,28 +85,53 @@
 ):
     gx = lax.axis_index("gx")
     gy = lax.axis_index("gy")
-    at_x = [lax.rem(gx // 4 + d, 4) * 4 for d in range(4)]
     at_z = [lax.rem(lax.rem(gx, 4) + d, 4) for d in range(4)]
     at_y = [lax.rem(gy // 2 + d, 4) * 2 for d in range(4)]
     at_c = [lax.rem(lax.rem(gy, 2) + d, 2) for d in range(2)]
 
-    def peer(slot):
-        dx, dz, dy, dc = OFFSETS[slot]
-        return (at_x[dx] + at_z[dz], at_y[dy] + at_c[dc])
+    def row_of(chunk):
+        offset = lax.rem(jnp.where(chunk < 2, 2 - chunk, chunk + 1), 4)
+        return lax.rem(gx // 4 + offset, 4) * 4
+
+    def peer(base, i):
+        dz, dy, dc = OFFSETS[i]
+        return (base + at_z[dz], at_y[dy] + at_c[dc])
+
+    def each(body):
+        def one(chunk, carry):
+            body(chunk)
+            return carry
+
+        lax.fori_loop(0, CHUNKS, one, 0)
 
     barrier = pltpu.get_barrier_semaphore()
 
-    for slot in range(PEERS - 1):
-        pl.semaphore_signal(barrier, inc=1, device_id=peer(slot), device_id_type=MESH)
+    @each
+    def greet(chunk):
+        base = row_of(chunk)
+        for i in range(PER):
+
+            def signal(i=i):
+                pl.semaphore_signal(barrier, inc=1, device_id=peer(base, i), device_id_type=MESH)
+
+            if i < PER - 1:
+                signal()
+            else:
+                pl.when(chunk < CHUNKS - 1)(signal)
 
     lane = lax.broadcasted_iota(jnp.int32, (1, LANES), 1)
-    for slot in range(PEERS):
-        ox, oy = peer(slot)
-        owner = ox * 8 + oy
-        cell_row[slot : slot + 1, :] = local_ref[pl.ds(owner, 1), :]
-        send_i[slot, 0:1, :] = remote_ref[pl.ds(owner, 1), :]
-        mult = mult_ref[pl.ds(owner, 1), :]
-        send_a[slot, 1:2, :] = jnp.where(lane < count_ref[0, owner], mult, 0.0)
+
+    @each
+    def order(chunk):
+        base = row_of(chunk)
+        for i in range(PER):
+            slot = chunk * PER + i
+            ox, oy = peer(base, i)
+            owner = ox * 8 + oy
+            cell_row[pl.ds(slot, 1), :] = local_ref[pl.ds(owner, 1), :]
+            send_a[slot, 2:3, :] = remote_ref[pl.ds(owner, 1), :].astype(F32)
+            mult = mult_ref[pl.ds(owner, 1), :]
+            send_a[slot, 1:2, :] = jnp.where(lane < count_ref[0, owner], mult, 0.0)
 
     keff[...] = jnp.where(active_ref[...] != 0, perm_ref[...], 0.0)
     diag_acc[...] = jnp.where(active_ref[...] != 0, acc_ref[...], 1.0)
@@ -126,9 +140,9 @@
     across = lax.broadcasted_iota(jnp.int32, (LANES, LANES), 1)
 
     def index_lanes(kind, chunk):
-        cells = cell_row[chunk * PER : (chunk + 1) * PER, :]
-        base = chunk * 2 * PER + kind * PER
-        lo_ref[base : base + PER, :] = (
+        cells = cell_row[pl.ds(pl.multiple_of(chunk * PER, PER), PER), :]
+        base = pl.multiple_of(chunk * 2 * PER + kind * PER, PER)
+        lo_ref[pl.ds(base, PER), :] = (
             ((cells >> 12) * 2 + ((cells >> 8) & 1)) * 8 + ((cells >> 9) & 7)
         )
 
@@ -146,18 +160,10 @@
         turned[...] = jnp.transpose(cell_row[...] & 255)
 
         def some(step, carry):
-            for i in range(4):
-                slot = step * 4 + i
-                pick = jnp.full((8, LANES), slot, jnp.int32)
-                column = jnp.concatenate(
-                    [
-                        jnp.take_along_axis(
-                            turned[8 * j : 8 * j + 8, :], pick, axis=1, mode="promise_in_bounds"
-                        )
-                        for j in range(16)
-                    ],
-                    axis=0,
-                )
+            shifted = pltpu.roll(turned[...], lax.rem(LANES - step * 16, LANES), 1)
+            for i in range(16):
+                slot = step * 16 + i
+                column = jnp.broadcast_to(shifted[:, i : i + 1], (LANES, LANES))
                 place = (slot // PER) * 2 * PER + kind * PER + lax.rem(slot, PER)
                 start = pl.multiple_of(place * LANES, LANES)
                 for half in range(2):
@@ -166,7 +172,7 @@
                     ).astype(BF16)
             return carry
 
-        lax.fori_loop(0, PEERS // 4, some, 0)
+        lax.fori_loop(0, PEERS // 16, some, 0)
 
     def set_table(values):
         for a in range(4):
@@ -206,21 +212,34 @@
         )
 
     def send(phase, chunk, source, target):
-        for slot in range(chunk * PER, (chunk + 1) * PER):
-            if slot < PEERS - 1:
-                back = MIRROR[slot]
+        base = row_of(chunk)
+        back_chunk = jnp.where(jnp.logical_and(chunk > 0, chunk < 3), 3 - chunk, chunk)
+        for i in range(PER):
+            slot = chunk * PER + i
+
+            def away(i=i, slot=slot):
                 pltpu.make_async_remote_copy(
                     src_ref=source.at[slot],
-                    dst_ref=target.at[back],
+                    dst_ref=target.at[back_chunk * PER + MIRROR[i]],
                     send_sem=ssem.at[phase],
-                    recv_sem=rsem.at[phase, back // PER],
-                    device_id=peer(slot),
+                    recv_sem=rsem.at[phase, back_chunk],
+                    device_id=peer(base, i),
                     device_id_type=MESH,
                 ).start()
 
+            if i < PER - 1:
+                away()
+            else:
+                pl.when(chunk < CHUNKS - 1)(away)
+
+                @pl.when(chunk == CHUNKS - 1)
+                def here(slot=slot):
+                    pltpu.make_async_copy(
+                        source.at[slot], target.at[slot], rsem.at[phase, chunk]
+                    ).start()
+
     def wait_chunk(phase, chunk, target):
-        count = PER - 1 if chunk == CHUNKS - 1 else PER
-        block = target.at[pl.ds(chunk * PER, count)]
+        block = target.at[pl.ds(chunk * PER, PER)]
         pltpu.make_async_copy(block, block, rsem.at[phase, chunk]).wait()
 
     def wait_sent(phase, source):
@@ -272,38 +291,39 @@
         return plane, (east, west, north, south, above, below)
 
     set_table(keff)
-    for chunk in range(CHUNKS):
-
-        def put_k(i, row, chunk=chunk):
+
+    @each
+    def own_ends(chunk):
+        def put_k(i, row):
             send_a[chunk * PER + i, 0:1, :] = row
 
         index_lanes(0, chunk)
         gather(chunk * 2 * PER, PER, put_k)
+
     index_rows(0)
 
     pl.semaphore_wait(barrier, PEERS - 1)
 
-    for chunk in range(CHUNKS):
-        send(0, chunk, send_i, recv_i)
+    @each
+    def send_ends(chunk):
+        send(0, chunk, send_a, recv_a)
+
     send_faces(0, keff)
-    for chunk in range(CHUNKS):
-        send(1, chunk, send_a, recv_a)
-    recv_i[PEERS - 1] = send_i[PEERS - 1]
-    recv_a[PEERS - 1] = send_a[PEERS - 1]
-
-    for chunk in range(CHUNKS):
-        wait_chunk(0, chunk, recv_i)
+
+    @each
+    def asked_ends(chunk):
+        wait_chunk(0, chunk, recv_a)
         for i in range(PER):
             slot = chunk * PER + i
-            cell_row[slot : slot + 1, :] = recv_i[slot, 0:1, :]
+            cell_row[pl.ds(slot, 1), :] = recv_a[slot, 2:3, :].astype(jnp.int32)
         index_lanes(1, chunk)
 
-        def put_k(i, row, chunk=chunk):
+        def put_k(i, row):
             send_b[chunk * PER + i, 0:1, :] = row
 
         gather(chunk * 2 * PER + PER, PER, put_k)
-        send(2, chunk, send_b, recv_b)
-    recv_b[PEERS - 1] = send_b[PEERS - 1]
+        send(1, chunk, send_b, recv_b)
+
     index_rows(1)
     for copy in face_copies(0):
         copy.wait_recv()
@@ -328,33 +348,32 @@
             amount = amount + one
         diagonal[a] = amount
 
-    total = jnp.zeros((128, 256), F32)
-    for chunk in range(CHUNKS):
-        wait_chunk(1, chunk, recv_a)
+    def asked_trans(chunk, total):
+        first = chunk * 2 * PER + PER
+
+        def value(i):
+            slot = chunk * PER + i
+            one = harmonic(recv_a[slot, 0:1, :], send_b[slot, 0:1, :], 1.0) * recv_a[slot, 1:2, :]
+            fault_trans[pl.ds(first + i, 1), :] = one
+            return one
+
+        return scatter(first, PER, value, total)
+
+    def own_trans(chunk, total):
+        wait_chunk(1, chunk, recv_b)
         first = chunk * 2 * PER
 
-        def asked(i, chunk=chunk, first=first):
+        def value(i):
             slot = chunk * PER + i
-            value = (
-                harmonic(recv_a[slot, 0:1, :], send_b[slot, 0:1, :], 1.0) * recv_a[slot, 1:2, :]
-            )
-            fault_trans[first + PER + i : first + PER + i + 1, :] = value
-            return value
-
-        total = scatter(first + PER, PER, asked, total)
-    for chunk in range(CHUNKS):
-        wait_chunk(2, chunk, recv_b)
-        first = chunk * 2 * PER
-
-        def owned(i, chunk=chunk, first=first):
-            slot = chunk * PER + i
-            value = (
-                harmonic(send_a[slot, 0:1, :], recv_b[slot, 0:1, :], 1.0) * send_a[slot, 1:2, :]
-            )
-            fault_trans[first + i : first + i + 1, :] = value
-            return value
-
-        total = scatter(first, PER, owned, total)
+            one = harmonic(send_a[slot, 0:1, :], recv_b[slot, 0:1, :], 1.0) * send_a[slot, 1:2, :]
+            fault_trans[pl.ds(first + i, 1), :] = one
+            return one
+
+        return scatter(first, PER, value, total)
+
+    nothing = jnp.zeros((128, 256), F32)
+    total = lax.fori_loop(0, CHUNKS, asked_trans, nothing)
+    total = lax.fori_loop(0, CHUNKS, own_trans, total)
 
     def place(total, a):
         halves = [
@@ -376,20 +395,22 @@
         corr_ref[a] = jnp.zeros((8, 512), F32)
 
     def iteration(count, rho):
-        phase = count + 3
+        phase = count + 2
         face_phase = count + 1
         send_faces(face_phase, step_ref)
         set_table(step_ref)
         source, target = send_p.at[count], recv_p.at[count]
-        for chunk in range(CHUNKS):
+
+        @each
+        def ask(chunk):
             for kind in range(2):
 
-                def put_p(i, row, chunk=chunk, kind=kind):
+                def put_p(i, row, kind=kind):
                     source[chunk * PER + i, kind : kind + 1, :] = row
 
                 gather(chunk * 2 * PER + kind * PER, PER, put_p)
             send(phase, chunk, source, target)
-        target[PEERS - 1] = source[PEERS - 1]
+
         for copy in face_copies(face_phase):
             copy.wait_recv()
         for a in range(4):
@@ -399,18 +420,20 @@
                 result = result + trans[side, a] * (plane - others[side])
             corr_ref[a] = corr_ref[a] + plane
             grid_part[a] = result
-        total = jnp.zeros((128, 256), F32)
-        for chunk in range(CHUNKS):
+
+        def answer(chunk, total):
             wait_chunk(phase, chunk, target)
             first = chunk * 2 * PER
 
-            def flux(i, chunk=chunk, first=first):
+            def flux(i):
                 slot, kind = chunk * PER + i % PER, i // PER
-                return fault_trans[first + i : first + i + 1, :] * (
+                return fault_trans[pl.ds(first + i, 1), :] * (
                     source[slot, kind : kind + 1, :] - target[slot, 1 - kind : 2 - kind, :]
                 )
 
-            total = scatter(first, 2 * PER, flux, total)
+            return scatter(first, 2 * PER, flux, total)
+
+        total = lax.fori_loop(0, CHUNKS, answer, nothing)
         rho_new = 1.0 / (2.0 * sigma - rho)
         for a in range(4):
             resid = resid_ref[a] - (grid_part[a] + place(total, a))
@@ -419,7 +442,7 @@
         return rho_new
 
     lax.fori_loop(0, ITERS, iteration, 1.0 / sigma)
-    sent = [send_i, send_a, send_b] + [send_p.at[count] for count in range(ITERS)]
+    sent = [send_a, send_b] + [send_p.at[count] for count in range(ITERS)]
     for phase, source in enumerate(sent):
         wait_sent(phase, source)
     for phase in range(ITERS + 1):
@@ -464,10 +487,8 @@
                 pltpu.VMEM((rows, LANES), F32),
                 pltpu.VMEM((LANES, LANES), jnp.int32),
                 cells,
-                pltpu.VMEM((PEERS, 1, LANES), jnp.int32),
-                pltpu.VMEM((PEERS, 1, LANES), jnp.int32),
-                pltpu.VMEM((PEERS, 2, LANES), F32),
-                pltpu.VMEM((PEERS, 2, LANES), F32),
+                pltpu.VMEM((PEERS, 3, LANES), F32),
+                pltpu.VMEM((PEERS, 3, LANES), F32),
                 pltpu.VMEM((PEERS, 1, LANES), F32),
                 pltpu.VMEM((PEERS, 1, LANES), F32),
                 pltpu.VMEM((ITERS, PEERS, 2, LANES), F32),
@@ -476,8 +497,8 @@
                 pltpu.VMEM((ITERS + 1, 2, 8, 512), F32),
                 pltpu.VMEM((ITERS + 1, 2, 4, 512), F32),
                 pltpu.VMEM((ITERS + 1, 2, 4, 512), F32),
-                pltpu.SemaphoreType.DMA((ITERS + 3,)),
-                pltpu.SemaphoreType.DMA((ITERS + 3, CHUNKS)),
+                pltpu.SemaphoreType.DMA((ITERS + 2,)),
+                pltpu.SemaphoreType.DMA((ITERS + 2, CHUNKS)),
                 pltpu.SemaphoreType.DMA((ITERS + 1, 4)),
                 pltpu.SemaphoreType.DMA((ITERS + 1, 4)),
             ],

time: 82.9 us -> 70.3 us (0.85)
  Pallas kernels: 78.6 us -> 66 us
    pallas_call x1, Pallas kernels: 78.6 us -> 66 us  [on_device(): pl.pallas_call(kernel, out_shape=[jax.ShapeDtypeStruct(shape, F32)] * 2,...]
where the time goes in v3:
time: 70.3 us; the launch traced here: 70.1 us
  Pallas kernels  66 us (94%)
  local copies, waits for them, and re-layouts  2.14 us (3%)
  between operations  1.94 us (3%)
    pallas_call x1, Pallas kernels, on_device(): pl.pallas_call(kernel, out_shape=[jax.ShapeDtypeStruct(shape, F32)] * 2,...  66 us
    unnamed x4, local copies, waits for them, and re-layouts  2.14 us

profile of v3, /device:TPU:1, one launch (start us, length us, event | category | flops | bytes accessed | tf_op | source)
XLA Modules:
  0.0 70.1 jit_solution(6816745938624343105)
XLA Ops:
  1.9 66.0 %shard_map.113 = (f32[4,8,512]{2,1,0:T(8,128)}, f32[4,8,512]{2,1,0:T(8,128)}) custom-call(f32[4,8,512]{2,1,0:T(8,128)} %right_ref.1, f32[4,8,512]{2,1,0:T(8,128)} %perm_ref.1, f32[4,8,512]{2,1,0:T(8,128)} %acc_ref.1, s32[4,8,512]{2,1,0:T(8,128)} %active_ref.1, s32[128,128]{1,0:T(8,128)} %bitcast.7, s32[128,128]{1,0:T(8,128)} %bitcast.8, f32[128,128]{1,0:T(8,128)} %bitcast.9, ...), custom_call_target="tpu_custom_call" | custom-call | tf_op jit(solution)/shard_map/pallas_call | solution.py:471
  67.9 0.0 copy-start
  68.0 1.5 %copy.16 = f32[4,8,512]{2,1,0:T(8,128)} copy(f32[4,8,512]{2,1,0:T(8,128)} %get-tuple-element.4) | data formatting | bytes 131072
  69.5 0.0 copy-done
  69.5 0.6 copy.17
Async XLA Ops:
  67.9 1.5 %copy-start = (f32[4,8,512]{2,1,0:T(8,128)S(1)}, f32[4,8,512]{2,1,0:T(8,128)}, u32[]{:S(2)}) copy-start(f32[4,8,512]{2,1,0:T(8,128)} %get-tuple-element.5) | copy-start | bytes 196612

commit v4 on v3

--- a/solution.py
+++ b/solution.py
@@ -31,11 +31,22 @@
 
 def slot_plan():
     def hops(offset):
-        return sum(min(d, 4 - d) for d in offset[:2])
-
-    offsets = [(z, y, c) for z in range(4) for y in range(4) for c in range(2)]
-    offsets.sort(key=lambda offset: (-hops(offset), offset[0], offset[1], 1 - offset[2]))
-    mirror = [offsets.index((-z % 4, -y % 4, c)) for z, y, c in offsets]
+        return sum(min(d, 4 - d) for d in offset[:3])
+
+    def opposite(offset):
+        return tuple(-d % 4 for d in offset[:3]) + (offset[3],)
+
+    offsets = [(x, z, y, c) for x in range(4) for z in range(4) for y in range(4) for c in range(2)]
+
+    def rank(offset):
+        pair = min(offset[:3], opposite(offset)[:3])
+        alone = offset[:3] == opposite(offset)[:3]
+        first = alone if hops(offset) == 2 else not alone
+        return (-hops(offset), first, pair, offset[:3], 1 - offset[3])
+
+    offsets.sort(key=rank)
+    mirror = [offsets.index(opposite(offset)) for offset in offsets]
+    assert all(slot // PER == back // PER for slot, back in enumerate(mirror))
     return offsets, mirror
 
 
@@ -43,6 +54,18 @@
 
 
 def kernel(
+    right_in,
+    perm_in,
+    acc_in,
+    active_in,
+    local_in,
+    remote_in,
+    mult_in,
+    count_in,
+    low_in,
+    high_in,
+    corr_ref,
+    resid_ref,
     right_ref,
     perm_ref,
     acc_ref,
@@ -53,8 +76,7 @@
     count_ref,
     low_ref,
     high_ref,
-    corr_ref,
-    resid_ref,
+    in_sem,
     keff,
     diag_acc,
     diagonal,
@@ -89,13 +111,27 @@
     at_y = [lax.rem(gy // 2 + d, 4) * 2 for d in range(4)]
     at_c = [lax.rem(lax.rem(gy, 2) + d, 2) for d in range(2)]
 
-    def row_of(chunk):
-        offset = lax.rem(jnp.where(chunk < 2, 2 - chunk, chunk + 1), 4)
-        return lax.rem(gx // 4 + offset, 4) * 4
-
-    def peer(base, i):
-        dz, dy, dc = OFFSETS[i]
-        return (base + at_z[dz], at_y[dy] + at_c[dc])
+    at_x = [lax.rem(gx // 4 + d, 4) * 4 for d in range(4)]
+
+    def peer(slot):
+        dx, dz, dy, dc = OFFSETS[slot]
+        return (at_x[dx] + at_z[dz], at_y[dy] + at_c[dc])
+
+    pairs = (
+        (local_in, local_ref),
+        (remote_in, remote_ref),
+        (mult_in, mult_ref),
+        (count_in, count_ref),
+        (perm_in, perm_ref),
+        (active_in, active_ref),
+        (acc_in, acc_ref),
+        (right_in, right_ref),
+        (low_in, low_ref),
+        (high_in, high_ref),
+    )
+
+    def load(number):
+        return pltpu.make_async_copy(*pairs[number], in_sem.at[number])
 
     def each(body):
         def one(chunk, carry):
@@ -104,35 +140,27 @@
 
         lax.fori_loop(0, CHUNKS, one, 0)
 
+    for number in range(10):
+        load(number).start()
     barrier = pltpu.get_barrier_semaphore()
 
-    @each
-    def greet(chunk):
-        base = row_of(chunk)
-        for i in range(PER):
-
-            def signal(i=i):
-                pl.semaphore_signal(barrier, inc=1, device_id=peer(base, i), device_id_type=MESH)
-
-            if i < PER - 1:
-                signal()
-            else:
-                pl.when(chunk < CHUNKS - 1)(signal)
+    for slot in range(PEERS - 1):
+        pl.semaphore_signal(barrier, inc=1, device_id=peer(slot), device_id_type=MESH)
+
+    for number in (0, 1, 2, 3):
+        load(number).wait()
 
     lane = lax.broadcasted_iota(jnp.int32, (1, LANES), 1)
-
-    @each
-    def order(chunk):
-        base = row_of(chunk)
-        for i in range(PER):
-            slot = chunk * PER + i
-            ox, oy = peer(base, i)
-            owner = ox * 8 + oy
-            cell_row[pl.ds(slot, 1), :] = local_ref[pl.ds(owner, 1), :]
-            send_a[slot, 2:3, :] = remote_ref[pl.ds(owner, 1), :].astype(F32)
-            mult = mult_ref[pl.ds(owner, 1), :]
-            send_a[slot, 1:2, :] = jnp.where(lane < count_ref[0, owner], mult, 0.0)
-
+    for slot in range(PEERS):
+        ox, oy = peer(slot)
+        owner = ox * 8 + oy
+        cell_row[slot : slot + 1, :] = local_ref[pl.ds(owner, 1), :]
+        send_a[slot, 2:3, :] = remote_ref[pl.ds(owner, 1), :].astype(F32)
+        mult = mult_ref[pl.ds(owner, 1), :]
+        send_a[slot, 1:2, :] = jnp.where(lane < count_ref[0, owner], mult, 0.0)
+
+    for number in range(4, 10):
+        load(number).wait()
     keff[...] = jnp.where(active_ref[...] != 0, perm_ref[...], 0.0)
     diag_acc[...] = jnp.where(active_ref[...] != 0, acc_ref[...], 1.0)
 
@@ -176,18 +204,16 @@
 
     def set_table(values):
         for a in range(4):
-            for h in range(2):
-                row = (a * 2 + h) * 8
-                head, tail = split(values[a, :, h * 256 : h * 256 + 256])
-                table[row : row + 8, :] = head.astype(F32)
-                table[64 + row : 72 + row, :] = tail.astype(F32)
+            halves = jnp.concatenate([values[a, :, 0:256], values[a, :, 256:512]], axis=0)
+            head, tail = split(halves)
+            table[a * 16 : a * 16 + 16, :] = head
+            table[64 + a * 16 : 80 + a * 16, :] = tail
 
     def gather(first, count, write):
         down = lax.broadcasted_iota(jnp.int32, (64, LANES), 0)
         start = pl.multiple_of(first * LANES, LANES)
-        rows = table[...].astype(BF16)
         found = jnp.dot(
-            rows, hot_lanes[:, pl.ds(start, count * LANES)], preferred_element_type=F32
+            table[...], hot_lanes[:, pl.ds(start, count * LANES)], preferred_element_type=F32
         )
         for i in range(count):
             block = found[0:64, i * LANES : (i + 1) * LANES] + found[64:128, i * LANES : (i + 1) * LANES]
@@ -212,31 +238,25 @@
         )
 
     def send(phase, chunk, source, target):
-        base = row_of(chunk)
-        back_chunk = jnp.where(jnp.logical_and(chunk > 0, chunk < 3), 3 - chunk, chunk)
-        for i in range(PER):
-            slot = chunk * PER + i
-
-            def away(i=i, slot=slot):
-                pltpu.make_async_remote_copy(
-                    src_ref=source.at[slot],
-                    dst_ref=target.at[back_chunk * PER + MIRROR[i]],
-                    send_sem=ssem.at[phase],
-                    recv_sem=rsem.at[phase, back_chunk],
-                    device_id=peer(base, i),
-                    device_id_type=MESH,
-                ).start()
-
-            if i < PER - 1:
-                away()
-            else:
-                pl.when(chunk < CHUNKS - 1)(away)
-
-                @pl.when(chunk == CHUNKS - 1)
-                def here(slot=slot):
+        def part(number):
+            for slot in range(number * PER, (number + 1) * PER):
+                back = MIRROR[slot]
+                if slot < PEERS - 1:
+                    pltpu.make_async_remote_copy(
+                        src_ref=source.at[slot],
+                        dst_ref=target.at[back],
+                        send_sem=ssem.at[phase],
+                        recv_sem=rsem.at[phase, number],
+                        device_id=peer(slot),
+                        device_id_type=MESH,
+                    ).start()
+                else:
                     pltpu.make_async_copy(
-                        source.at[slot], target.at[slot], rsem.at[phase, chunk]
+                        source.at[slot], target.at[slot], rsem.at[phase, number]
                     ).start()
+
+        for number in range(CHUNKS):
+            pl.when(chunk == number)(functools.partial(part, number))
 
     def wait_chunk(phase, chunk, target):
         block = target.at[pl.ds(chunk * PER, PER)]
@@ -383,8 +403,8 @@
         ]
         return jnp.concatenate(halves, axis=1)
 
-    low = jnp.broadcast_to(low_ref[...], (8, 512))
-    high = jnp.broadcast_to(high_ref[...], (8, 512))
+    low = jnp.full((8, 512), low_ref[0], F32)
+    high = jnp.full((8, 512), high_ref[0], F32)
     theta = (high + low) / 2.0
     delta = (high - low) / 2.0
     sigma = theta / delta
@@ -403,12 +423,11 @@
 
         @each
         def ask(chunk):
-            for kind in range(2):
-
-                def put_p(i, row, kind=kind):
-                    source[chunk * PER + i, kind : kind + 1, :] = row
-
-                gather(chunk * 2 * PER + kind * PER, PER, put_p)
+            def put_p(i, row):
+                kind = i // PER
+                source[chunk * PER + i % PER, kind : kind + 1, :] = row
+
+            gather(chunk * 2 * PER, 2 * PER, put_p)
             send(phase, chunk, source, target)
 
         for copy in face_copies(face_phase):
@@ -464,16 +483,26 @@
 ):
     shape = right_side.shape
     vmem = pl.BlockSpec(memory_space=pltpu.VMEM)
-    smem = pl.BlockSpec(memory_space=pltpu.SMEM)
     rows = 2 * PEERS
     cells = pltpu.VMEM(shape, F32)
     return tuple(
         pl.pallas_call(
             kernel,
             out_shape=[jax.ShapeDtypeStruct(shape, F32)] * 2,
-            in_specs=[vmem] * 7 + [smem] + [vmem] * 2,
+            in_specs=[pl.BlockSpec(memory_space=pl.ANY)] * 10,
             out_specs=[vmem] * 2,
             scratch_shapes=[
+                cells,
+                cells,
+                cells,
+                pltpu.VMEM(shape, jnp.int32),
+                pltpu.VMEM((PEERS, LANES), jnp.int32),
+                pltpu.VMEM((PEERS, LANES), jnp.int32),
+                pltpu.VMEM((PEERS, LANES), F32),
+                pltpu.SMEM((1, PEERS), jnp.int32),
+                pltpu.SMEM((1,), F32),
+                pltpu.SMEM((1,), F32),
+                pltpu.SemaphoreType.DMA((10,)),
                 cells,
                 cells,
                 cells,
@@ -483,7 +512,7 @@
                 pltpu.VMEM((rows, LANES), jnp.int32),
                 pltpu.VMEM((256, rows * LANES), BF16),
                 pltpu.VMEM((rows * LANES, 256), BF16),
-                pltpu.VMEM((128, 256), F32),
+                pltpu.VMEM((128, 256), BF16),
                 pltpu.VMEM((rows, LANES), F32),
                 pltpu.VMEM((LANES, LANES), jnp.int32),
                 cells,
@@ -514,8 +543,8 @@
             fault_remote.reshape(PEERS, LANES),
             fault_mult.reshape(PEERS, LANES),
             fault_count,
-            low_bound.reshape(1, 1),
-            high_bound.reshape(1, 1),
+            low_bound,
+            high_bound,
         )
     )
 

time: 70.3 us -> 66.8 us (0.950)
  Pallas kernels: 66 us -> 62.6 us
    pallas_call x1, Pallas kernels: 66 us -> 62.6 us  [on_device(): pl.pallas_call(kernel, out_shape=[jax.ShapeDtypeStruct(shape, F32)] * 2,...]
where the time goes in v4:
time: 66.8 us; the launch traced here: 66.7 us
  Pallas kernels  62.6 us (94%)
  local copies, waits for them, and re-layouts  2.14 us (3%)
  between operations  1.94 us (3%)
    pallas_call x1, Pallas kernels, on_device(): pl.pallas_call(kernel, out_shape=[jax.ShapeDtypeStruct(shape, F32)] * 2,...  62.6 us
    unnamed x4, local copies, waits for them, and re-layouts  2.14 us

profile of v4, /device:TPU:1, one launch (start us, length us, event | category | flops | bytes accessed | tf_op | source)
XLA Modules:
  0.0 66.7 jit_solution(16641234432405593877)
XLA Ops:
  1.9 62.6 %shard_map.113 = (f32[4,8,512]{2,1,0:T(8,128)}, f32[4,8,512]{2,1,0:T(8,128)}) custom-call(f32[4,8,512]{2,1,0:T(8,128)} %right_in.1, f32[4,8,512]{2,1,0:T(8,128)} %perm_in.1, f32[4,8,512]{2,1,0:T(8,128)} %acc_in.1, s32[4,8,512]{2,1,0:T(8,128)} %active_in.1, s32[128,128]{1,0:T(8,128)} %bitcast.3, s32[128,128]{1,0:T(8,128)} %bitcast.4, f32[128,128]{1,0:T(8,128)} %bitcast.5, ...), custom_call_target="tpu_custom_call" | custom-call | tf_op jit(solution)/shard_map/pallas_call | solution.py:489
  64.5 0.0 copy-start
  64.5 1.5 %copy.16 = f32[4,8,512]{2,1,0:T(8,128)} copy(f32[4,8,512]{2,1,0:T(8,128)} %get-tuple-element.4) | data formatting | bytes 131072
  66.0 0.0 copy-done
  66.0 0.6 copy.17
Async XLA Ops:
  64.5 1.5 %copy-start = (f32[4,8,512]{2,1,0:T(8,128)S(1)}, f32[4,8,512]{2,1,0:T(8,128)}, u32[]{:S(2)}) copy-start(f32[4,8,512]{2,1,0:T(8,128)} %get-tuple-element.5) | copy-start | bytes 196612

commit v5 on v4

--- a/solution.py
+++ b/solution.py
@@ -9,7 +9,7 @@
 
 ITERS = 3
 PEERS = 128
-CHUNKS = 4
+CHUNKS = 2
 PER = PEERS // CHUNKS
 LANES = 128
 MESH = pl.DeviceIdType.MESH
@@ -113,9 +113,12 @@
 
     at_x = [lax.rem(gx // 4 + d, 4) * 4 for d in range(4)]
 
+    at_xz = [[x + z for z in at_z] for x in at_x]
+    at_yc = [[y + c for c in at_c] for y in at_y]
+
     def peer(slot):
         dx, dz, dy, dc = OFFSETS[slot]
-        return (at_x[dx] + at_z[dz], at_y[dy] + at_c[dc])
+        return (at_xz[dx][dz], at_yc[dy][dc])
 
     pairs = (
         (local_in, local_ref),
@@ -320,31 +323,16 @@
         index_lanes(0, chunk)
         gather(chunk * 2 * PER, PER, put_k)
 
-    index_rows(0)
 
     pl.semaphore_wait(barrier, PEERS - 1)
+
+    send_faces(0, keff)
 
     @each
     def send_ends(chunk):
         send(0, chunk, send_a, recv_a)
 
-    send_faces(0, keff)
-
-    @each
-    def asked_ends(chunk):
-        wait_chunk(0, chunk, recv_a)
-        for i in range(PER):
-            slot = chunk * PER + i
-            cell_row[pl.ds(slot, 1), :] = recv_a[slot, 2:3, :].astype(jnp.int32)
-        index_lanes(1, chunk)
-
-        def put_k(i, row):
-            send_b[chunk * PER + i, 0:1, :] = row
-
-        gather(chunk * 2 * PER + PER, PER, put_k)
-        send(1, chunk, send_b, recv_b)
-
-    index_rows(1)
+    index_rows(0)
     for copy in face_copies(0):
         copy.wait_recv()
 
@@ -368,6 +356,21 @@
             amount = amount + one
         diagonal[a] = amount
 
+    @each
+    def asked_ends(chunk):
+        wait_chunk(0, chunk, recv_a)
+        for i in range(PER):
+            slot = chunk * PER + i
+            cell_row[pl.ds(slot, 1), :] = recv_a[slot, 2:3, :].astype(jnp.int32)
+        index_lanes(1, chunk)
+
+        def put_k(i, row):
+            send_b[chunk * PER + i, 0:1, :] = row
+
+        gather(chunk * 2 * PER + PER, PER, put_k)
+        send(1, chunk, send_b, recv_b)
+
+    index_rows(1)
     def asked_trans(chunk, total):
         first = chunk * 2 * PER + PER
 

time: 66.8 us -> 62.9 us (0.942)
  Pallas kernels: 62.6 us -> 58.6 us
    pallas_call x1, Pallas kernels: 62.6 us -> 58.6 us  [on_device(): pl.pallas_call(kernel, out_shape=[jax.ShapeDtypeStruct(shape, F32)] * 2,...]
where the time goes in v5:
time: 62.9 us; the launch traced here: 62.7 us
  Pallas kernels  58.6 us (93%)
  local copies, waits for them, and re-layouts  2.14 us (3%)
  between operations  1.94 us (3%)
    pallas_call x1, Pallas kernels, on_device(): pl.pallas_call(kernel, out_shape=[jax.ShapeDtypeStruct(shape, F32)] * 2,...  58.6 us
    unnamed x4, local copies, waits for them, and re-layouts  2.14 us

profile of v5, /device:TPU:1, one launch (start us, length us, event | category | flops | bytes accessed | tf_op | source)
XLA Modules:
  0.0 62.7 jit_solution(3496631886352963278)
XLA Ops:
  1.9 58.6 %shard_map.113 = (f32[4,8,512]{2,1,0:T(8,128)}, f32[4,8,512]{2,1,0:T(8,128)}) custom-call(f32[4,8,512]{2,1,0:T(8,128)} %right_in.1, f32[4,8,512]{2,1,0:T(8,128)} %perm_in.1, f32[4,8,512]{2,1,0:T(8,128)} %acc_in.1, s32[4,8,512]{2,1,0:T(8,128)} %active_in.1, s32[128,128]{1,0:T(8,128)} %bitcast.3, s32[128,128]{1,0:T(8,128)} %bitcast.4, f32[128,128]{1,0:T(8,128)} %bitcast.5, ...), custom_call_target="tpu_custom_call" | custom-call | tf_op jit(solution)/shard_map/pallas_call | solution.py:492
  60.5 0.0 copy-start
  60.5 1.5 %copy.16 = f32[4,8,512]{2,1,0:T(8,128)} copy(f32[4,8,512]{2,1,0:T(8,128)} %get-tuple-element.4) | data formatting | bytes 131072
  62.0 0.0 copy-done
  62.1 0.6 %copy.17 = f32[4,8,512]{2,1,0:T(8,128)} copy(f32[4,8,512]{2,1,0:T(8,128)S(1)} %copy-done) | data formatting | bytes 131072
Async XLA Ops:
  60.5 1.5 %copy-start = (f32[4,8,512]{2,1,0:T(8,128)S(1)}, f32[4,8,512]{2,1,0:T(8,128)}, u32[]{:S(2)}) copy-start(f32[4,8,512]{2,1,0:T(8,128)} %get-tuple-element.5) | copy-start | bytes 196612

commit v6 on v5

--- a/solution.py
+++ b/solution.py
@@ -373,24 +373,26 @@
     index_rows(1)
     def asked_trans(chunk, total):
         first = chunk * 2 * PER + PER
+        slots = pl.ds(chunk * PER, PER)
+        fault_trans[pl.ds(first, PER), :] = (
+            harmonic(recv_a[slots, 0, :], send_b[slots, 0, :], 1.0) * recv_a[slots, 1, :]
+        )
 
         def value(i):
-            slot = chunk * PER + i
-            one = harmonic(recv_a[slot, 0:1, :], send_b[slot, 0:1, :], 1.0) * recv_a[slot, 1:2, :]
-            fault_trans[pl.ds(first + i, 1), :] = one
-            return one
+            return fault_trans[pl.ds(first + i, 1), :]
 
         return scatter(first, PER, value, total)
 
     def own_trans(chunk, total):
         wait_chunk(1, chunk, recv_b)
         first = chunk * 2 * PER
+        slots = pl.ds(chunk * PER, PER)
+        fault_trans[pl.ds(first, PER), :] = (
+            harmonic(send_a[slots, 0, :], recv_b[slots, 0, :], 1.0) * send_a[slots, 1, :]
+        )
 
         def value(i):
-            slot = chunk * PER + i
-            one = harmonic(send_a[slot, 0:1, :], recv_b[slot, 0:1, :], 1.0) * send_a[slot, 1:2, :]
-            fault_trans[pl.ds(first + i, 1), :] = one
-            return one
+            return fault_trans[pl.ds(first + i, 1), :]
 
         return scatter(first, PER, value, total)
 

time: 62.9 us -> 63 us (level)
  no operation moved by 1% of the time
where the time goes in v6:
time: 63 us; the launch traced here: 62.8 us
  Pallas kernels  58.7 us (93%)
  local copies, waits for them, and re-layouts  2.14 us (3%)
  between operations  1.94 us (3%)
    pallas_call x1, Pallas kernels, on_device(): pl.pallas_call(kernel, out_shape=[jax.ShapeDtypeStruct(shape, F32)] * 2,...  58.7 us
    unnamed x4, local copies, waits for them, and re-layouts  2.14 us

profile of v6, /device:TPU:1, one launch (start us, length us, event | category | flops | bytes accessed | tf_op | source)
XLA Modules:
  0.0 62.8 jit_solution(17027408888519491586)
XLA Ops:
  1.9 58.7 %shard_map.113 = (f32[4,8,512]{2,1,0:T(8,128)}, f32[4,8,512]{2,1,0:T(8,128)}) custom-call(f32[4,8,512]{2,1,0:T(8,128)} %right_in.1, f32[4,8,512]{2,1,0:T(8,128)} %perm_in.1, f32[4,8,512]{2,1,0:T(8,128)} %acc_in.1, s32[4,8,512]{2,1,0:T(8,128)} %active_in.1, s32[128,128]{1,0:T(8,128)} %bitcast.3, s32[128,128]{1,0:T(8,128)} %bitcast.4, f32[128,128]{1,0:T(8,128)} %bitcast.5, ...), custom_call_target="tpu_custom_call" | custom-call | tf_op jit(solution)/shard_map/pallas_call | solution.py:494
  60.6 0.0 copy-start
  60.7 1.5 %copy.16 = f32[4,8,512]{2,1,0:T(8,128)} copy(f32[4,8,512]{2,1,0:T(8,128)} %get-tuple-element.4) | data formatting | bytes 131072
  62.2 0.0 copy-done
  62.2 0.6 %copy.17 = f32[4,8,512]{2,1,0:T(8,128)} copy(f32[4,8,512]{2,1,0:T(8,128)S(1)} %copy-done) | data formatting | bytes 131072
Async XLA Ops:
  60.6 1.5 %copy-start = (f32[4,8,512]{2,1,0:T(8,128)S(1)}, f32[4,8,512]{2,1,0:T(8,128)}, u32[]{:S(2)}) copy-start(f32[4,8,512]{2,1,0:T(8,128)} %get-tuple-element.5) | copy-start | bytes 196612
